TPU v7x, 256 devices: a whole 4x4x8 slice. The times are simulated.
256 devices in a mesh: group: 8 (over y, core), shard: 32 (over x, z).
Axes of the slice: x: 4, y: 4, z: 8, core: 2. Of those that a mesh axis runs over, the one named last changes fastest.
Arguments:
- query_states: bfloat16 [16384, 32, 1024], P(('group', 'shard')), may hold values from -6 to 6
- passage_states: bfloat16 [1024, 128, 1024], P(('group', 'shard')), may hold values from -6 to 6
- index_rows: bfloat16 [524288, 1024], P(('group', 'shard')), may hold values from -15 to 15
- weight: bfloat16 [1024, 1024], P('group'), may hold values from -0.1875 to 0.1875
- prev_weight: bfloat16 [1024, 1024], P('group'), may hold values from -0.1875 to 0.1875
- neg_owner: int32 [16384, 8, 1], P(('group', 'shard')), may hold values from 0 to 31; in each aligned block of 512 rows (0 to 511, 512 to 1023, ..., all dimensions but the last counted through in order) at most 32 rows name the same one
- neg_row: int32 [16384, 8], P(('group', 'shard')), may hold values from 0 to 2047
- positive: int32 [16384], P(('group', 'shard')), may hold values from 0 to 127
Outputs:
- grad_weight: float32 [1024, 1024], P('shard')
- query_loss: float32 [16384], P(('group', 'shard'))
- reencoded_document_embeddings: bfloat16 [1024, 1024], P(('group', 'shard'))
Inputs may be any that keep to these rules, and one draw needn't show every extreme that they name: `neg_owner`: in the rows of one device no shard is named more than 32 times, a bound that some block reaches.
All inputs are finite; a program needn't handle non-finite values.
Results may differ from a plain program's by a relative error of at most 0.0065.
Values may be sent and summed in bfloat16 or wider, within the bound.
A program may use at most 64 MiB of HBM per device.

v0:
```python
import math

import jax
import jax.numpy as jnp
from jax import lax
from jax.sharding import PartitionSpec as P

logit_divisor = 0.05


def shards(
    query_states, passage_states, index_rows, weight, prev_weight, neg_owner, neg_row, positive
):
    partition_number = lax.axis_size("shard")
    cluster_number = lax.axis_size("group")
    question_device_embeddings, q_len, width = query_states.shape
    p_local, p_len, _ = passage_states.shape
    neg_count = neg_row.shape[1]
    capacity = 2 * question_device_embeddings * neg_count // partition_number
    multiplier_coefficient = 1.0 / (
        logit_divisor * math.sqrt(question_device_embeddings * partition_number * cluster_number)
    )
    full_weight, full_prev = (
        lax.all_gather(weight, "group", axis=0, tiled=True),
        lax.all_gather(prev_weight, "group", axis=0, tiled=True),
    )
    passage_hidden = jnp.tanh(
        jnp.dot(
            passage_states.reshape(p_local * p_len, width),
            full_prev,
            preferred_element_type=jnp.float32,
        )
    )
    reencoded_document_embeddings = jnp.mean(
        passage_hidden.reshape(p_local, p_len, width), axis=1
    ).astype(jnp.bfloat16)
    batch_local_scores = lax.all_gather(reencoded_document_embeddings, "shard", axis=0, tiled=True)
    p_group = batch_local_scores.shape[0]
    owner_ids = neg_owner.reshape(-1)
    row_ids = neg_row.reshape(-1)
    owner_hot = (
        owner_ids[:, None] == jnp.arange(partition_number, dtype=jnp.int32)[None, :]
    ).astype(jnp.int32)
    before = jnp.cumsum(owner_hot, axis=0) - owner_hot
    slot_rank = jnp.sum(before * owner_hot, axis=1)
    slot_index = owner_ids * capacity + slot_rank
    request = (
        jnp.zeros((partition_number * capacity,), jnp.int32)
        .at[slot_index]
        .set(row_ids)
        .reshape(partition_number, capacity)
    )
    found_rows = jnp.take(
        index_rows,
        lax.all_to_all(request, "shard", split_axis=0, concat_axis=0, tiled=True),
        axis=0,
    )
    answered = lax.all_to_all(found_rows, "shard", split_axis=0, concat_axis=0, tiled=True)
    distractor_embeddings = answered.reshape(partition_number * capacity, width)[
        slot_index
    ].reshape(question_device_embeddings, neg_count, width)
    flat_queries = query_states.reshape(question_device_embeddings * q_len, width)
    hidden = jnp.tanh(
        jnp.dot(flat_queries, full_weight, preferred_element_type=jnp.float32)
    ).reshape(question_device_embeddings, q_len, width)
    question_embedding = jnp.mean(hidden, axis=1).astype(jnp.bfloat16)
    within_minibatch_similarity = (
        jnp.dot(question_embedding, batch_local_scores.T, preferred_element_type=jnp.float32)
        / logit_divisor
    )
    distractor_similarity = (
        jnp.einsum(
            "mz,mfz->mf",
            question_embedding,
            distractor_embeddings,
            preferred_element_type=jnp.float32,
        )
        / logit_divisor
    )
    logits = jnp.concatenate([within_minibatch_similarity, distractor_similarity], axis=1)
    row_max = jnp.max(logits, axis=1, keepdims=True)
    exp_terms = jnp.exp(logits - row_max)
    row_total = jnp.sum(exp_terms, axis=1, keepdims=True)
    softmax_w = exp_terms / row_total
    label_hot = (jnp.arange(p_group, dtype=jnp.int32)[None, :] == positive[:, None]).astype(
        jnp.float32
    )
    picked = jnp.sum(within_minibatch_similarity * label_hot, axis=1)
    query_loss = jnp.log(row_total[:, 0]) + row_max[:, 0] - picked
    coeff_in = (softmax_w[:, :p_group] - label_hot).astype(jnp.bfloat16)
    coeff_neg = softmax_w[:, p_group:].astype(jnp.bfloat16)
    query_grad = jnp.dot(coeff_in, batch_local_scores, preferred_element_type=jnp.float32)
    query_grad = query_grad + jnp.einsum(
        "qn,qnd->qd", coeff_neg, distractor_embeddings, preferred_element_type=jnp.float32
    )
    query_grad = query_grad * multiplier_coefficient
    hidden_grad = ((1.0 - hidden * hidden) * (query_grad[:, None, :] / q_len)).astype(jnp.bfloat16)
    partial_grad = jnp.einsum(
        "td,te->de",
        flat_queries,
        hidden_grad.reshape(question_device_embeddings * q_len, width),
        preferred_element_type=jnp.float32,
    )
    shard_sum = lax.psum_scatter(partial_grad, "shard", scatter_dimension=0, tiled=True)
    grad_weight = lax.psum(shard_sum, "group")
    return (grad_weight, query_loss, reencoded_document_embeddings)


def solution(mesh):
    return jax.shard_map(
        shards,
        mesh=mesh,
        in_specs=(
            P(("group", "shard"), None, None),
            P(("group", "shard"), None, None),
            P(("group", "shard"), None),
            P("group", None),
            P("group", None),
            P(("group", "shard"), None, None),
            P(("group", "shard"), None),
            P(("group", "shard")),
        ),
        out_specs=(P("shard", None), P(("group", "shard")), P(("group", "shard"), None)),
        check_vma=False,
    )
```

profile of v0, /device:TPU:1, one launch (start us, length us, event | category | flops | bytes accessed | tf_op | source)
XLA Modules:
  0.0 483.1 jit_solution(10800604473040355755)
XLA Ops:
  7.2 0.7 all-gather.6.cloned.1.call-update
  8.0 0.7 all-gather.4.cloned.1.call-update
  8.7 0.7 broadcast_multiply_fusion.1
  9.4 0.8 copy.27
  10.5 1.2 reduce-window.6
  12.1 0.8 copy.30
  12.9 2.4 scatter_custom_fusion
  15.5 20.3 %all_to_all.20 = s32[32,1,32]{2,1,0:T(1,128)S(1)} all-to-all(s32[32,1,32]{2,1,0:T(1,128)S(1)} %all_to_all.13), channel_id=1, replica_groups=mesh['group'=8,'shard'=32] {'shard'}, dimensions={0} | all-to-all | bytes 8192 | tf_op jit(solution)/shard_map/all_to_all | solution.py:55
  35.9 7.7 %gather_fusion = bf16[1024,1024]{1,0:T(8,128)(2,1)S(1)} fusion(bf16[2048,1024]{1,0:T(8,128)(2,1)} %param.10, s32[1024]{0:T(1024)S(1)} %broadcast_clamp_fusion), kind=kCustom, calls=%fused_computation | custom fusion | bytes 4198400 | tf_op jit(solution)/shard_map/jit(_take)/gather | solution.py:53
  43.6 1.6 broadcast_select_fusion
  45.2 4.0 all-to-all-start.1
  49.3 2.9 bitcast_reduce_fusion
  52.2 77.9 %all-gather = bf16[32,4,1024]{2,1,0:T(4,128)(2,1)} all-gather(bf16[1,4,1024]{2,1,0:T(4,128)(2,1)S(1)} %fusion.43), channel_id=1, replica_groups=mesh['group'=8,'shard'=32] {'shard'}, dimensions={0}, use_global_device_ids=true | all-gather | bytes 270336 | tf_op jit(solution)/shard_map/all_gather | solution.py:37
  130.1 1.0 reshape.155
  131.1 10.9 %bitcast_reduce_fusion.1 = (f32[64,1024]{1,0:T(8,128)S(1)}, f32[2048,1024]{1,0:T(8,128)}) fusion(bf16[2048,1024]{1,0:T(8,128)(2,1)} %bitcast.75, bf16[1024,1024]{1,0:T(8,128)(2,1)} %all-gather.4.cloned.1.call-done), kind=kOutput, calls=%fused_computation.59 | convolution fusion | flops 4296998912 | bytes 14942208 | tf_op jit(solution)/shard_map/dot_general | solution.py:64
  143.0 3.0 gather_fusion.1
  146.0 2.1 fusion.16
  148.6 1.6 fusion.14
  150.5 20.5 %fusion.8 = f32[1024,1024]{0,1:T(8,128)} fusion(bf16[64,32,1024]{2,1,0:T(8,128)(2,1)S(1)} %copy-done.2, f32[64,32,1024]{2,1,0:T(8,128)} %bitcast.76, f32[64,1024]{1,0:T(8,128)S(1)} %fusion.13), kind=kOutput, calls=%fused_computation.12 | convolution fusion | flops 4303355904 | bytes 17039360 | tf_op jit(solution)/shard_map/td,te->de/dot_general | solution.py:98
  171.0 5.3 %copy.37 = f32[1024,1024]{1,0:T(8,128)} copy(f32[1024,1024]{0,1:T(8,128)} %fusion.8) | data formatting | bytes 8388608
  177.0 228.2 %reduce-scatter.4.cloned.1.call-done = f32[32,1024]{1,0:T(8,128)} async-done(((f32[1024,1024]{1,0:T(8,128)}), f32[32,1024]{1,0:T(8,128)}) %reduce-scatter.4.cloned.1.call-update) | async-done | bytes 131088
  405.2 1.9 copy.38
  407.6 67.0 %all-reduce.2.cloned.1.call-done = f32[32,1024]{0,1:T(8,128)} async-done(((f32[32,1024]{0,1:T(8,128)}), f32[32,1024]{0,1:T(8,128)}) %all-reduce.2.cloned.1.call-update) | async-done | bytes 131088 | tf_op jit(solution)/shard_map/psum | solution.py:105
  474.7 1.9 copy.32
  (43 shorter events, 4.0 us)
Async XLA Ops:
  7.2 42.1 %copy-start = (bf16[4,128,1024]{2,1,0:T(8,128)(2,1)S(1)}, bf16[4,128,1024]{2,1,0:T(8,128)(2,1)}, u32[]{:S(2)}) copy-start(bf16[4,128,1024]{2,1,0:T(8,128)(2,1)} %param.9) | copy-start | bytes 3145732
  7.2 42.1 %all-gather.6.cloned.1.call-start = ((), (), s32[]{:S(2)}) async-start(), calls=%async_computation.4 | async-start | bytes 2359296 | tf_op jit(solution)/shard_map/all_gather | solution.py:25
  7.9 123.2 %all-gather.4.cloned.1.call-start = ((), (), s32[]{:S(2)}) async-start(), calls=%async_computation.3 | async-start | bytes 2359296 | tf_op jit(solution)/shard_map/all_gather | solution.py:24
  45.2 97.8 %all-to-all-start.1 = ((bf16[32,32,1024]{2,1,0:T(8,128)(2,1)}), bf16[32,32,1024]{2,1,0:T(8,128)(2,1)S(1)}, u32[]{:S(2)}, u32[]{:S(2)}) async-start(bf16[32,32,1024]{2,1,0:T(8,128)(2,1)} %broadcast_select_fusion), calls=%async_computation.1 | async-start | bytes 4194304 | tf_op jit(solution)/shard_map/all_to_all | solution.py:58
  49.2 356.0 %reduce-scatter.4.cloned.1.call-start = ((), (), s32[]{:S(2)}) async-start(), calls=%async_computation.6 | async-start | bytes 4325376
  131.1 11.5 %copy-start.1 = (s32[64]{0:T(128)S(1)}, s32[64]{0:T(128)}, u32[]{:S(2)}) copy-start(s32[64]{0:T(128)} %param.15) | copy-start | bytes 772
  146.0 4.4 copy-start.2
  176.3 298.3 %all-reduce.2.cloned.1.call-start = ((), (), s32[]{:S(2)}) async-start(), calls=%async_computation.5 | async-start | bytes 1048576 | tf_op jit(solution)/shard_map/psum | solution.py:105
Sparse Core Ops, SparseCore 0:
  9.9 31.9 all-gather.5
  43.7 28.0 all-gather.3
  176.5 228.6 reduce-scatter.3
  407.5 67.1 all-reduce.1
where the time goes:
time: 485 us; the launch traced here: 483 us
  waiting for transfers between devices  297 us (61%)
  blocking collectives  98.2 us (20%)
  matrix products  38.5 us (8%)
  local copies, waits for them, and re-layouts  25.8 us (5%)
  between operations  14 us (3%)
  other arithmetic  5.83 us (1%)
    unnamed x5, waiting for transfers between devices  230 us
    all_gather x1, blocking collectives, shards(): lax.all_gather(reencoded_document_embeddings, 'shard', axis=0, tiled=True)  77.9 us
    psum x1, waiting for transfers between devices, shards(): grad_weight = lax.psum(shard_sum, 'group')  67 us
    dot_general x1, matrix products, shards(): jnp.einsum('td,te->de', flat_queries, hidden_grad.reshape(question_device...  20.5 us
    all_to_all x1, blocking collectives, shards(): lax.all_to_all(request, 'shard', split_axis=0, concat_axis=0, tiled=True)  20.3 us
    unnamed x12, local copies, waits for them, and re-layouts  11.7 us
    dot_general x1, matrix products, shards(): jnp.dot(flat_queries, full_weight, preferred_element_type=jnp.float32)  10.9 us
  transfers between devices with their start and end apart: 5, of which 2 were waited for; matrix products, arithmetic and copies ran while one was open for 7% of the time, Pallas kernels for 0%

commit v1 on v0

v1 whole, which is shorter than its diff:
```python
import functools
import math

import jax
import jax.numpy as jnp
from jax import lax
from jax.experimental import pallas as pl
from jax.experimental.pallas import tpu as pltpu
from jax.sharding import PartitionSpec as P

MESH = pl.DeviceIdType.MESH
BF = jnp.bfloat16
F32 = jnp.float32

logit_divisor = 0.05

D = 1024
QD = 64
QL = 32
PD = 4
PL = 128
NEG = 8
ROWS = 2048
CAP = 32
NY, NC, NX, NZ = 4, 2, 4, 8
NG, NS = NY * NC, NX * NZ
TOK = QD * QL
SLOTS = NS * CAP
GRAD_SCALE = 1.0 / (logit_divisor * math.sqrt(QD * NS * NG))


def iota(shape, axis):
    return lax.broadcasted_iota(jnp.int32, shape, axis)


def to_column(row, n):
    eye = iota((n, n), 0) == iota((n, n), 1)
    return jnp.sum(jnp.where(eye, row, jnp.zeros_like(row)), axis=1, keepdims=True)


def to_row(column, n):
    eye = iota((n, n), 0) == iota((n, n), 1)
    return jnp.sum(jnp.where(eye, column, jnp.zeros_like(column)), axis=0, keepdims=True)


def kernel(
    owner_ref, row_ref, pos_ref, x_hbm, p_hbm, idx_hbm, w_hbm, pw_hbm,
    grad_ref, loss_ref, emb_ref,
    x_v, xt_v, p_v, idx_v, wp_v, ww_v,
    req_s, req_l, found, answer, mask_v,
    emb_f, emb_s, emb_l, e_v,
    d1_v, qv_f, qv_v, s_v, qg_v, hg_v,
    ex_s, ex_l, own_v, acc_a, acc_b, a_s, b_s, a_l, b_l,
    a2_s, b2_s, a2_l, b2_l, a2_o, b2_o, z_s, z_l, z_o, f_s, f_l,
    loc_sem, req_ss, req_rs, row_ss, row_rs, wp_ss, wp_rs, ww_ss, ww_rs,
    fp_ss, fw_ss, emb_ss, emb_rs, ex_ss, ex_rs, a_ss, a_rs, b_ss, b_rs,
    a2_ss, a2_rs, b2_ss, b2_rs, z_ss, z_rs, f_ss, f_rs,
):
    g, s = lax.axis_index("group"), lax.axis_index("shard")
    y, c = g // NC, g % NC
    x, z = s // NZ, s % NZ
    sib = y * NC + 1 - c

    def local(src, dst, k):
        return pltpu.make_async_copy(src, dst, loc_sem.at[k])

    def remote(src, dst, ss, rs, gg, sh):
        return pltpu.make_async_remote_copy(
            src_ref=src, dst_ref=dst, send_sem=ss, recv_sem=rs,
            device_id=(gg, sh), device_id_type=MESH,
        )

    def wait_in(dst, rs):
        remote(dst, dst, rs, rs, sib, s).wait_recv()

    def wait_out(src, ss):
        remote(src, src, ss, ss, sib, s).wait_send()

    barrier = pltpu.get_barrier_semaphore()

    @pl.loop(1, NS)
    def _(k):
        pl.semaphore_signal(barrier, inc=1, device_id=(g, (s + k) % NS), device_id_type=MESH)

    @pl.loop(1, NG)
    def _(k):
        pl.semaphore_signal(barrier, inc=1, device_id=((g + k) % NG, s), device_id_type=MESH)

    local_copies = [
        local(idx_hbm, idx_v, 0),
        local(pw_hbm, wp_v.at[g], 1),
        local(w_hbm, ww_v.at[g], 2),
        local(x_hbm, x_v, 3),
        local(p_hbm, p_v, 4),
    ]
    for copy in local_copies:
        copy.start()

    owners, rows = owner_ref[...], row_ref[...]
    lane = iota((QD, 128), 1)
    lower = (iota((QD, QD), 0) > iota((QD, QD), 1)).astype(F32).astype(BF)
    slot_lane = iota((QD, SLOTS), 1)
    base = jnp.zeros((1, 128), F32)
    mask = jnp.zeros((QD, SLOTS), F32)
    requests = jnp.zeros((128, 128), F32)
    for n in range(NEG):
        owner = owners[:, n : n + 1]
        hot = (lane == owner).astype(F32)
        before = jnp.dot(lower, hot.astype(BF), preferred_element_type=F32) + base
        rank = jnp.sum(hot * before, axis=1, keepdims=True).astype(jnp.int32)
        base = base + jnp.sum(hot, axis=0, keepdims=True)
        mask = mask + (slot_lane == owner * CAP + rank).astype(F32)
        row = rows[:, n : n + 1]
        here = lane == rank + (s % 4) * CAP
        high = jnp.where(here, row // 16, 0).astype(F32).astype(BF)
        low = jnp.where(here, row % 16, 0).astype(F32).astype(BF)
        hot_t = hot.T.astype(BF)
        requests = requests + (
            16.0 * jnp.dot(hot_t, high, preferred_element_type=F32)
            + jnp.dot(hot_t, low, preferred_element_type=F32)
        )
    mask_v[...] = mask
    for o in range(NS):
        req_s[o] = requests[o : o + 1, :]

    pl.semaphore_wait(barrier, NS - 1 + NG - 1)

    @pl.loop(1, NS)
    def _(k):
        o = (s + k) % NS
        remote(req_s.at[o], req_l.at[s], req_ss.at[o], req_rs.at[s], g, o).start()

    req_l[s] = req_s[s]

    for hbm, buf, ss, rs in ((pw_hbm, wp_v, wp_ss, wp_rs), (w_hbm, ww_v, ww_ss, ww_rs)):

        @pl.loop(1, NY)
        def _(k):
            peer = ((y + k) % NY) * NC + c
            remote(hbm, buf.at[g], ss.at[k], rs.at[g], peer, s).start()

        remote(hbm, buf.at[g], ss.at[0], rs.at[g], sib, s).start()

    @pl.loop(1, NS)
    def _(k):
        o = (s + k) % NS
        wait_in(req_l.at[o], req_rs.at[o])

    local_copies[0].wait()
    row_lane = iota((128, ROWS), 1)

    @pl.loop(0, NX)
    def _(i):
        xx = (x + 1 + i) % NX
        hots = []
        for half in range(NZ // 4):
            first = xx * NZ + half * 4
            ids = req_l[first] + req_l[first + 1] + req_l[first + 2] + req_l[first + 3]
            column = to_column(ids, 128).astype(jnp.int32)
            hots.append((row_lane == column).astype(F32).astype(BF))
        hot = jnp.concatenate(hots, axis=0)
        got = jnp.dot(hot, idx_v[...], preferred_element_type=F32).astype(BF)
        found[pl.ds(xx * NZ, NZ)] = got.reshape(NZ, CAP, D)

        @pl.loop(0, NZ)
        def _(k):
            r = xx * NZ + (z + 1 + k) % NZ

            @pl.when(r != s)
            def _():
                remote(found.at[r], answer.at[s], row_ss.at[r], row_rs.at[s], g, r).start()

    answer[s] = found[s]

    local_copies[3].wait()

    @pl.loop(0, TOK // 256)
    def _(i):
        at = pl.multiple_of(i * 256, 256)
        xt_v[:, pl.ds(at, 256)] = x_v[pl.ds(at, 256), :].T

    def gather_rest(buf, rs, fs):
        @pl.loop(1, NY)
        def _(k):
            peer = ((y + k) % NY) * NC + c
            wait_in(buf.at[peer], rs.at[peer])
            remote(buf.at[peer], buf.at[peer], fs.at[k], rs.at[peer], sib, s).start()

        @pl.loop(0, NY)
        def _(k):
            peer = k * NC + 1 - c
            wait_in(buf.at[peer], rs.at[peer])

    local_copies[1].wait()
    local_copies[4].wait()
    gather_rest(wp_v, wp_rs, fp_ss)
    for i in range(PD // 2):
        hidden = jnp.tanh(
            jnp.dot(
                p_v[i * 2 * PL : (i + 1) * 2 * PL, :],
                wp_v[...].reshape(D, D),
                preferred_element_type=F32,
            )
        )
        for j in range(2):
            mean = jnp.sum(hidden[j * PL : (j + 1) * PL], axis=0, keepdims=True) * (1.0 / PL)
            p = i * 2 + j
            for b in range(8):
                emb_f[b * PD + p : b * PD + p + 1, :] = mean[:, b * 128 : (b + 1) * 128]
    emb = emb_f[...].astype(BF)
    emb_s[...] = emb
    emb_l[s] = emb
    for b in range(8):
        emb_ref[:, b * 128 : (b + 1) * 128] = emb_f[b * PD : (b + 1) * PD, :].astype(BF)

    @pl.loop(1, NS)
    def _(k):
        o = (s + k) % NS
        remote(emb_s, emb_l.at[s], emb_ss.at[o], emb_rs.at[s], g, o).start()

    local_copies[2].wait()
    gather_rest(ww_v, ww_rs, fw_ss)

    @pl.loop(0, TOK // 256)
    def _(i):
        at = pl.multiple_of(i * 256, 256)
        hidden = jnp.tanh(
            jnp.dot(x_v[pl.ds(at, 256), :], ww_v[...].reshape(D, D), preferred_element_type=F32)
        )
        d1_v[pl.ds(at, 256), :] = 1.0 - hidden * hidden
        q_at = pl.multiple_of(i * 8, 8)
        qv_f[pl.ds(q_at, 8), :] = jnp.sum(hidden.reshape(8, QL, D), axis=1) * (1.0 / QL)

    qv_v[...] = qv_f[...].astype(BF)

    @pl.loop(1, NS)
    def _(k):
        o = (s + k) % NS
        wait_in(emb_l.at[o], emb_rs.at[o])

    pieces = emb_l[...].reshape(NS * 32, 128)
    to_passage, from_piece = iota((128, NS * 32), 0), iota((128, NS * 32), 1)
    for b in range(8):
        pick = (from_piece == (to_passage // PD) * 32 + b * PD + to_passage % PD)
        e_v[:, b * 128 : (b + 1) * 128] = jnp.dot(
            pick.astype(F32).astype(BF), pieces, preferred_element_type=F32
        ).astype(BF)

    nt = (((1,), (1,)), ((), ()))
    in_logits = (
        lax.dot_general(qv_v[...], e_v[...], nt, preferred_element_type=F32) / logit_divisor
    )

    @pl.loop(0, NX)
    def _(i):
        xx = (x + 2 * NX - 1 - i) % NX

        @pl.loop(0, NZ)
        def _(k):
            o = xx * NZ + (z + NZ + NZ - 1 - k) % NZ

            @pl.when(o != s)
            def _():
                wait_in(answer.at[o], row_rs.at[o])

        got = answer[pl.ds(xx * NZ, NZ)].reshape(NZ * CAP, D)
        s_v[:, pl.ds(pl.multiple_of(xx * NZ * CAP, NZ * CAP), NZ * CAP)] = lax.dot_general(
            qv_v[...], got, nt, preferred_element_type=F32
        )

    named = mask_v[...] > 0.5
    neg_logits = jnp.where(named, s_v[...] / logit_divisor, -jnp.inf)
    top = jnp.maximum(
        jnp.max(in_logits, axis=1, keepdims=True), jnp.max(neg_logits, axis=1, keepdims=True)
    )
    in_exp = jnp.exp(in_logits - top)
    neg_exp = jnp.where(named, jnp.exp(neg_logits - top), 0.0)
    total = jnp.sum(in_exp, axis=1, keepdims=True) + jnp.sum(neg_exp, axis=1, keepdims=True)
    label = (iota((QD, 128), 1) == to_column(pos_ref[...].astype(F32), QD).astype(jnp.int32))
    label = label.astype(F32)
    picked = jnp.sum(in_logits * label, axis=1, keepdims=True)
    loss_ref[...] = to_row(jnp.log(total) + top - picked, QD)
    coeff_in = (in_exp / total - label).astype(BF)
    coeff_neg = (neg_exp / total).astype(BF)
    query_grad = jnp.dot(coeff_in, e_v[...], preferred_element_type=F32) + jnp.dot(
        coeff_neg, answer[...].reshape(SLOTS, D), preferred_element_type=F32
    )
    qg_v[...] = query_grad * GRAD_SCALE * (1.0 / QL)

    @pl.loop(0, QD // 8)
    def _(i):
        q_at = pl.multiple_of(i * 8, 8)
        grads = qg_v[pl.ds(q_at, 8), :]
        for j in range(8):
            at = pl.multiple_of(i * 256 + j * QL, QL)
            value = (d1_v[pl.ds(at, QL), :] * grads[j : j + 1, :]).astype(BF)
            hg_v[0, pl.ds(at, QL), :] = value[:, : D // 2]
            hg_v[1, pl.ds(at, QL), :] = value[:, D // 2 :]

    def finish(i):
        xx = (x + 1 + i) % NX
        wait_in(ex_l.at[i], ex_rs.at[i])
        both = own_v[i % 2] + ex_l[i].astype(F32)
        both = both.reshape(NZ, 2, 16, D // 2)
        part_a = both[:, 0].reshape(NZ * 16, D // 2)
        part_b = both[:, 1].reshape(NZ * 16, D // 2)
        acc_b[xx] = part_b
        b_s[xx] = part_b.astype(BF)
        for k in range(NY):
            piece = part_a[:, k * 128 : (k + 1) * 128]
            acc_a[k, xx] = piece
            a_s[k, xx] = piece.astype(BF)

        @pl.when(i < NX - 1)
        def _():
            remote(b_s.at[xx], b_l.at[i], b_ss.at[i], b_rs.at[i], g, xx * NZ + z).start()

        @pl.loop(1, NY)
        def _(k):
            yy = (y + k) % NY
            remote(
                a_s.at[yy, xx], a_l.at[k - 1, xx], a_ss.at[k - 1, i], a_rs.at[k - 1, i],
                yy * NC + c, s,
            ).start()

    @pl.loop(0, NX)
    def _(i):
        xx = (x + 1 + i) % NX
        left = xt_v[pl.ds(pl.multiple_of(xx * 256, 256), 256), :]
        ex_s[i] = jnp.dot(left, hg_v[1 - c], preferred_element_type=F32).astype(BF)
        remote(ex_s.at[i], ex_l.at[i], ex_ss.at[i], ex_rs.at[i], sib, s).start()

        @pl.when(i > 0)
        def _():
            finish(i - 1)

        own_v[i % 2] = jnp.dot(left, hg_v[c], preferred_element_type=F32)

    finish(NX - 1)

    @pl.loop(0, NX)
    def _(i):
        xx = (x + 1 + i) % NX
        part = acc_a[y, xx]
        for k in range(1, NY):
            wait_in(a_l.at[k - 1, xx], a_rs.at[k - 1, i])
            part = part + a_l[k - 1, xx].astype(F32)

        @pl.when(i < NX - 1)
        def _():
            a2_s[i] = part.astype(BF)
            remote(a2_s.at[i], a2_l.at[i], a2_ss.at[i], a2_rs.at[i], g, xx * NZ + z).start()

        @pl.when(i == NX - 1)
        def _():
            a2_o[...] = part

    part_b = acc_b[x]
    for k in range(NX - 1):
        wait_in(b_l.at[k], b_rs.at[k])
        part_b = part_b + b_l[k].astype(F32)
    for k in range(NY):
        piece = part_b[:, k * 128 : (k + 1) * 128]
        b2_o[k] = piece
        b2_s[k] = piece.astype(BF)

    @pl.loop(1, NY)
    def _(k):
        yy = (y + k) % NY
        remote(b2_s.at[yy], b2_l.at[k - 1], b2_ss.at[k - 1], b2_rs.at[k - 1], yy * NC + c, s).start()

    part_a = a2_o[...]
    for k in range(NX - 1):
        wait_in(a2_l.at[k], a2_rs.at[k])
        part_a = part_a + a2_l[k].astype(F32)
    part_b = b2_o[y]
    for k in range(NY - 1):
        wait_in(b2_l.at[k], b2_rs.at[k])
        part_b = part_b + b2_l[k].astype(F32)
    part_a = part_a.reshape(NZ, 16, 128)
    part_b = part_b.reshape(NZ, 16, 128)
    z_o[:, 0:16, :] = part_a
    z_o[:, 16:32, :] = part_b
    z_s[...] = z_o[...].astype(BF)

    @pl.loop(1, NZ)
    def _(k):
        zz = (z + k) % NZ
        remote(z_s.at[zz], z_l.at[k - 1], z_ss.at[k - 1], z_rs.at[k - 1], g, x * NZ + zz).start()

    total_part = z_o[z]
    for k in range(NZ - 1):
        wait_in(z_l.at[k], z_rs.at[k])
        total_part = total_part + z_l[k].astype(F32)

    f_s[...] = total_part
    f_l[g] = total_part

    @pl.loop(1, NG)
    def _(k):
        gg = (g + k) % NG
        remote(f_s, f_l.at[g], f_ss.at[k], f_rs.at[g], gg, s).start()

    @pl.loop(1, NG)
    def _(k):
        gg = (g + k) % NG
        wait_in(f_l.at[gg], f_rs.at[gg])

    for yy in range(NY):
        for cc in range(NC):
            at = (cc * NY + yy) * 128
            grad_ref[:, at : at + 128] = f_l[yy * NC + cc]

    @pl.loop(1, NS)
    def _(k):
        o = (s + k) % NS
        wait_out(req_s.at[o], req_ss.at[o])
        wait_out(found.at[o], row_ss.at[o])
        wait_out(emb_s, emb_ss.at[o])

    for buf, ss, fs in ((wp_v, wp_ss, fp_ss), (ww_v, ww_ss, fw_ss)):

        @pl.loop(0, NY)
        def _(k):
            wait_out(buf.at[g], ss.at[k])

        @pl.loop(1, NY)
        def _(k):
            wait_out(buf.at[((y + k) % NY) * NC + c], fs.at[k])

    @pl.loop(0, NX)
    def _(i):
        wait_out(ex_s.at[i], ex_ss.at[i])

        @pl.loop(0, NY - 1)
        def _(k):
            wait_out(a_s.at[0, 0], a_ss.at[k, i])

    @pl.loop(0, NX - 1)
    def _(i):
        wait_out(b_s.at[i], b_ss.at[i])
        wait_out(a2_s.at[i], a2_ss.at[i])

    @pl.loop(0, NY - 1)
    def _(i):
        wait_out(b2_s.at[i], b2_ss.at[i])

    @pl.loop(0, NZ - 1)
    def _(i):
        wait_out(z_s.at[i], z_ss.at[i])

    @pl.loop(1, NG)
    def _(k):
        wait_out(f_s, f_ss.at[k])


def shards(
    query_states, passage_states, index_rows, weight, prev_weight, neg_owner, neg_row, positive
):
    vmem = pl.BlockSpec(memory_space=pltpu.VMEM)
    hbm = pl.BlockSpec(memory_space=pl.ANY)
    dma = pltpu.SemaphoreType.DMA
    half = D // 2
    scratch = [
        pltpu.VMEM((TOK, D), BF),
        pltpu.VMEM((D, TOK), BF),
        pltpu.VMEM((PD * PL, D), BF),
        pltpu.VMEM((ROWS, D), BF),
        pltpu.VMEM((NG, D // NG, D), BF),
        pltpu.VMEM((NG, D // NG, D), BF),
        pltpu.VMEM((NS, 1, 128), F32),
        pltpu.VMEM((NS, 1, 128), F32),
        pltpu.VMEM((NS, CAP, D), BF),
        pltpu.VMEM((NS, CAP, D), BF),
        pltpu.VMEM((QD, SLOTS), F32),
        pltpu.VMEM((32, 128), F32),
        pltpu.VMEM((32, 128), BF),
        pltpu.VMEM((NS, 32, 128), BF),
        pltpu.VMEM((NS * PD, D), BF),
        pltpu.VMEM((TOK, D), F32),
        pltpu.VMEM((QD, D), F32),
        pltpu.VMEM((QD, D), BF),
        pltpu.VMEM((QD, SLOTS), F32),
        pltpu.VMEM((QD, D), F32),
        pltpu.VMEM((2, TOK, half), BF),
        pltpu.VMEM((NX, 256, half), BF),
        pltpu.VMEM((NX, 256, half), BF),
        pltpu.VMEM((2, 256, half), F32),
        pltpu.VMEM((NY, NX, 128, 128), F32),
        pltpu.VMEM((NX, 128, half), F32),
        pltpu.VMEM((NY, NX, 128, 128), BF),
        pltpu.VMEM((NX, 128, half), BF),
        pltpu.VMEM((NY - 1, NX, 128, 128), BF),
        pltpu.VMEM((NX - 1, 128, half), BF),
        pltpu.VMEM((NX - 1, 128, 128), BF),
        pltpu.VMEM((NY, 128, 128), BF),
        pltpu.VMEM((NX - 1, 128, 128), BF),
        pltpu.VMEM((NY - 1, 128, 128), BF),
        pltpu.VMEM((128, 128), F32),
        pltpu.VMEM((NY, 128, 128), F32),
        pltpu.VMEM((NZ, 32, 128), BF),
        pltpu.VMEM((NZ - 1, 32, 128), BF),
        pltpu.VMEM((NZ, 32, 128), F32),
        pltpu.VMEM((32, 128), F32),
        pltpu.VMEM((NG, 32, 128), F32),
        dma((5,)),
        dma((NS,)), dma((NS,)),
        dma((NS,)), dma((NS,)),
        dma((NY,)), dma((NG,)),
        dma((NY,)), dma((NG,)),
        dma((NY,)), dma((NY,)),
        dma((NS,)), dma((NS,)),
        dma((NX,)), dma((NX,)),
        dma((NY - 1, NX)), dma((NY - 1, NX)),
        dma((NX - 1,)), dma((NX - 1,)),
        dma((NX - 1,)), dma((NX - 1,)),
        dma((NY - 1,)), dma((NY - 1,)),
        dma((NZ - 1,)), dma((NZ - 1,)),
        dma((NG,)), dma((NG,)),
    ]
    grad, loss, emb = pl.pallas_call(
        kernel,
        out_shape=(
            jax.ShapeDtypeStruct((D // NS, D), F32),
            jax.ShapeDtypeStruct((1, QD), F32),
            jax.ShapeDtypeStruct((PD, D), BF),
        ),
        in_specs=[vmem] * 3 + [hbm] * 5,
        out_specs=(vmem, vmem, vmem),
        scratch_shapes=scratch,
        compiler_params=pltpu.CompilerParams(
            collective_id=0, has_side_effects=True, vmem_limit_bytes=60 << 20
        ),
        cost_estimate=pl.CostEstimate(
            flops=16 * 2**30, bytes_accessed=12 * 2**20, transcendentals=3 * 2**20
        ),
        name="retriever_step",
    )(
        neg_owner.reshape(QD, NEG),
        neg_row,
        positive.reshape(1, QD),
        query_states.reshape(TOK, D),
        passage_states.reshape(PD * PL, D),
        index_rows,
        weight,
        prev_weight,
    )
    return grad, loss.reshape(QD), emb


def solution(mesh):
    return jax.shard_map(
        shards,
        mesh=mesh,
        in_specs=(
            P(("group", "shard"), None, None),
            P(("group", "shard"), None, None),
            P(("group", "shard"), None),
            P("group", None),
            P("group", None),
            P(("group", "shard"), None, None),
            P(("group", "shard"), None),
            P(("group", "shard")),
        ),
        out_specs=(P("shard", None), P(("group", "shard")), P(("group", "shard"), None)),
        check_vma=False,
    )
```

time: 485 us -> 112 us (0.23)
  waiting for transfers between devices: 297 us -> 0 us
  Pallas kernels: 0 us -> 105 us
  blocking collectives: 98.2 us -> 0 us
  matrix products: 38.5 us -> 0 us
  local copies, waits for them, and re-layouts: 25.8 us -> 6.8 us
  between operations: 14 us -> 0.64 us
  other arithmetic: 5.83 us -> 0 us
    unnamed x5 -> x0, waiting for transfers between devices: 230 us -> none
    pallas_call x0 -> x1, Pallas kernels: none -> 105 us  [shards(): pl.pallas_call(kernel, out_shape=(jax.ShapeDtypeStruct((D // NS, D), F32)...]
    all_gather x1 -> x0, blocking collectives: 77.9 us -> none  [shards(): lax.all_gather(reencoded_document_embeddings, 'shard', axis=0, tiled=True)]
    psum x1 -> x0, waiting for transfers between devices: 67 us -> none  [shards(): grad_weight = lax.psum(shard_sum, 'group')]
    dot_general x7 -> x0, matrix products: 38.5 us -> none  [the longest x1 20.5 us: shards(): jnp.einsum('td,te->de', flat_queries, hidden_grad.reshape(question_device...]
    all_to_all x1 -> x0, blocking collectives: 20.3 us -> none  [shards(): lax.all_to_all(request, 'shard', split_axis=0, concat_axis=0, tiled=True)]
    gather x2 -> x0, local copies, waits for them, and re-layouts: 10.8 us -> none  [the longest x1 7.75 us: shards(): jnp.take(index_rows, lax.all_to_all(request, 'shard', split_axis=0, conca...]
    unnamed x12 -> x5, local copies, waits for them, and re-layouts: 11.7 us -> 6.8 us
  transfers between devices with their start and end apart: 5 -> 0, of which waited for: 2 -> 0; matrix products, arithmetic and copies ran while one was open for 7% -> 0% of each run, Pallas kernels for 0% -> 0%
where the time goes in v1:
time: 112 us
  Pallas kernels  105 us (94%)
  local copies, waits for them, and re-layouts  6.8 us (6%)
    pallas_call x1, Pallas kernels, shards(): pl.pallas_call(kernel, out_shape=(jax.ShapeDtypeStruct((D // NS, D), F32)...  105 us
    unnamed x5, local copies, waits for them, and re-layouts  6.8 us

profile of v1, /device:TPU:1, one launch (start us, length us, event | category | flops | bytes accessed | tf_op | source)
XLA Modules:
  0.0 111.9 jit_solution(9092480977422286090)
XLA Ops:
  0.6 1.4 %copy.11 = s32[64,8,1]{1,0,2:T(8,128)} copy(s32[64,8,1]{0,2,1:T(1,128)} %param.13) | data formatting | bytes 4096 | tf_op args[5]
  2.0 1.4 %copy.12.row_ref = s32[64,8]{1,0:T(8,128)} copy(s32[64,8]{0,1:T(8,128)} %param.14) | data formatting | bytes 4096 | tf_op args[6]
  3.4 104.5 %retriever_step.1 = (f32[32,1024]{1,0:T(8,128)}, f32[1,64]{1,0:T(1,128)}, bf16[4,1024]{1,0:T(4,128)(2,1)}) custom-call(s32[64,8]{1,0:T(8,128)} %bitcast.5, s32[64,8]{1,0:T(8,128)} %copy.12.row_ref, s32[1,64]{1,0:T(1,128)} %bitcast.8, bf16[2048,1024]{1,0:T(8,128)(2,1)} %bitcast.6, bf16[512,1024]{1,0:T(8,128)(2,1)} %bitcast.7, bf16[2048,1024]{1,0:T(8,128)(2,1)} %idx_hbm.1, ...), custom_call_target="tpu_custom_call" | custom-call | flops 17179869184 | bytes 12582912 | tf_op jit(solution)/shard_map/retriever_step/pallas_call | solution.py:521
  107.9 1.6 %copy.16 = f32[32,1024]{1,0:T(8,128)} copy(f32[32,1024]{1,0:T(8,128)} %get-tuple-element.12) | data formatting | bytes 262144
  109.5 1.2 %copy.17 = f32[64]{0:T(128)} copy(f32[64]{0:T(128)} %bitcast.9) | data formatting | bytes 512
  110.6 1.3 %copy.18 = bf16[4,1024]{1,0:T(4,128)(2,1)} copy(bf16[4,1024]{1,0:T(4,128)(2,1)} %get-tuple-element.14) | data formatting | bytes 16384

commit v2 on v1

--- a/solution.py
+++ b/solution.py
@@ -26,6 +26,7 @@
 NG, NS = NY * NC, NX * NZ
 TOK = QD * QL
 SLOTS = NS * CAP
+RA, RB = 5 * 32, 3 * 32
 GRAD_SCALE = 1.0 / (logit_divisor * math.sqrt(QD * NS * NG))
 
 
@@ -44,16 +45,16 @@
 
 
 def kernel(
-    owner_ref, row_ref, pos_ref, x_hbm, p_hbm, idx_hbm, w_hbm, pw_hbm,
+    owner_hbm, row_hbm, pos_hbm, x_hbm, p_hbm, idx_hbm, w_hbm, pw_hbm,
     grad_ref, loss_ref, emb_ref,
-    x_v, xt_v, p_v, idx_v, wp_v, ww_v,
+    owner_ref, row_ref, pos_ref, x_v, xt_v, p_v, idx_v, wp_v, ww_v,
     req_s, req_l, found, answer, mask_v,
     emb_f, emb_s, emb_l, e_v,
     d1_v, qv_f, qv_v, s_v, qg_v, hg_v,
     ex_s, ex_l, own_v, acc_a, acc_b, a_s, b_s, a_l, b_l,
     a2_s, b2_s, a2_l, b2_l, a2_o, b2_o, z_s, z_l, z_o, f_s, f_l,
     loc_sem, req_ss, req_rs, row_ss, row_rs, wp_ss, wp_rs, ww_ss, ww_rs,
-    fp_ss, fw_ss, emb_ss, emb_rs, ex_ss, ex_rs, a_ss, a_rs, b_ss, b_rs,
+    fp_ss, fw_ss, emb_ss, emb_rs, line_ss, line_rs, ex_ss, ex_rs, a_ss, a_rs, b_ss, b_rs,
     a2_ss, a2_rs, b2_ss, b2_rs, z_ss, z_rs, f_ss, f_rs,
 ):
     g, s = lax.axis_index("group"), lax.axis_index("shard")
@@ -75,6 +76,16 @@
 
     def wait_out(src, ss):
         remote(src, src, ss, ss, sib, s).wait_send()
+
+    nt = (((1,), (1,)), ((), ()))
+
+    small_copies = [
+        local(owner_hbm, owner_ref, 5),
+        local(row_hbm, row_ref, 6),
+        local(pos_hbm, pos_ref, 7),
+    ]
+    for copy in small_copies:
+        copy.start()
 
     barrier = pltpu.get_barrier_semaphore()
 
@@ -96,30 +107,28 @@
     for copy in local_copies:
         copy.start()
 
-    owners, rows = owner_ref[...], row_ref[...]
-    lane = iota((QD, 128), 1)
-    lower = (iota((QD, QD), 0) > iota((QD, QD), 1)).astype(F32).astype(BF)
-    slot_lane = iota((QD, SLOTS), 1)
-    base = jnp.zeros((1, 128), F32)
-    mask = jnp.zeros((QD, SLOTS), F32)
-    requests = jnp.zeros((128, 128), F32)
+    for copy in small_copies:
+        copy.wait()
+    upper = (iota((QD, QD), 0) < iota((QD, QD), 1)).astype(F32).astype(BF)
+    base = jnp.zeros((NS, 1), F32)
+    requests = jnp.zeros((NS, 128), F32)
+    slots = []
     for n in range(NEG):
-        owner = owners[:, n : n + 1]
-        hot = (lane == owner).astype(F32)
-        before = jnp.dot(lower, hot.astype(BF), preferred_element_type=F32) + base
-        rank = jnp.sum(hot * before, axis=1, keepdims=True).astype(jnp.int32)
-        base = base + jnp.sum(hot, axis=0, keepdims=True)
-        mask = mask + (slot_lane == owner * CAP + rank).astype(F32)
-        row = rows[:, n : n + 1]
-        here = lane == rank + (s % 4) * CAP
+        owner = owner_ref[n]
+        hot = (iota((NS, QD), 0) == owner).astype(F32)
+        hot_bf = hot.astype(BF)
+        before = jnp.dot(hot_bf, upper, preferred_element_type=F32) + base
+        rank = jnp.sum(hot * before, axis=0, keepdims=True).astype(jnp.int32)
+        base = base + jnp.sum(hot, axis=1, keepdims=True)
+        slots.append((owner * CAP + rank).astype(F32))
+        row = row_ref[n : n + 1, :]
+        here = iota((128, QD), 0) == rank + (s % 4) * CAP
         high = jnp.where(here, row // 16, 0).astype(F32).astype(BF)
         low = jnp.where(here, row % 16, 0).astype(F32).astype(BF)
-        hot_t = hot.T.astype(BF)
         requests = requests + (
-            16.0 * jnp.dot(hot_t, high, preferred_element_type=F32)
-            + jnp.dot(hot_t, low, preferred_element_type=F32)
+            16.0 * lax.dot_general(hot_bf, high, nt, preferred_element_type=F32)
+            + lax.dot_general(hot_bf, low, nt, preferred_element_type=F32)
         )
-    mask_v[...] = mask
     for o in range(NS):
         req_s[o] = requests[o : o + 1, :]
 
@@ -141,17 +150,32 @@
 
         remote(hbm, buf.at[g], ss.at[0], rs.at[g], sib, s).start()
 
-    @pl.loop(1, NS)
-    def _(k):
-        o = (s + k) % NS
-        wait_in(req_l.at[o], req_rs.at[o])
-
     local_copies[0].wait()
     row_lane = iota((128, ROWS), 1)
 
+    def send_rows(i):
+        xx = (x + i) % NX
+
+        @pl.loop(0, NZ)
+        def _(k):
+            r = xx * NZ + (z + 1 + k) % NZ
+
+            @pl.when(r != s)
+            def _():
+                remote(found.at[r], answer.at[s], row_ss.at[r], row_rs.at[s], g, r).start()
+
     @pl.loop(0, NX)
     def _(i):
-        xx = (x + 1 + i) % NX
+        xx = (x + i) % NX
+
+        @pl.loop(0, NZ)
+        def _(k):
+            r = xx * NZ + (z + 1 + k) % NZ
+
+            @pl.when(r != s)
+            def _():
+                wait_in(req_l.at[r], req_rs.at[r])
+
         hots = []
         for half in range(NZ // 4):
             first = xx * NZ + half * 4
@@ -162,15 +186,17 @@
         got = jnp.dot(hot, idx_v[...], preferred_element_type=F32).astype(BF)
         found[pl.ds(xx * NZ, NZ)] = got.reshape(NZ, CAP, D)
 
-        @pl.loop(0, NZ)
-        def _(k):
-            r = xx * NZ + (z + 1 + k) % NZ
-
-            @pl.when(r != s)
-            def _():
-                remote(found.at[r], answer.at[s], row_ss.at[r], row_rs.at[s], g, r).start()
+        @pl.when(i < NX // 2)
+        def _():
+            send_rows(i)
 
     answer[s] = found[s]
+
+    slot_lane = iota((QD, SLOTS), 1)
+    mask = jnp.zeros((QD, SLOTS), F32)
+    for n in range(NEG):
+        mask = mask + (slot_lane == to_column(slots[n], QD).astype(jnp.int32)).astype(F32)
+    mask_v[...] = mask
 
     local_copies[3].wait()
 
@@ -213,13 +239,29 @@
     for b in range(8):
         emb_ref[:, b * 128 : (b + 1) * 128] = emb_f[b * PD : (b + 1) * PD, :].astype(BF)
 
-    @pl.loop(1, NS)
-    def _(k):
-        o = (s + k) % NS
-        remote(emb_s, emb_l.at[s], emb_ss.at[o], emb_rs.at[s], g, o).start()
+    @pl.loop(1, NZ)
+    def _(k):
+        zz = (z + k) % NZ
+        remote(emb_s, emb_l.at[s], emb_ss.at[k], emb_rs.at[z], g, x * NZ + zz).start()
+
+    send_rows(2)
 
     local_copies[2].wait()
     gather_rest(ww_v, ww_rs, fw_ss)
+
+    @pl.loop(1, NZ)
+    def _(k):
+        zz = (z + k) % NZ
+        wait_in(emb_l.at[x * NZ + zz], emb_rs.at[zz])
+
+    line = emb_l.at[pl.ds(x * NZ, NZ)]
+
+    @pl.loop(1, NX)
+    def _(k):
+        xx = (x + k) % NX
+        remote(line, line, line_ss.at[k], line_rs.at[x], g, xx * NZ + z).start()
+
+    send_rows(3)
 
     @pl.loop(0, TOK // 256)
     def _(i):
@@ -233,10 +275,28 @@
 
     qv_v[...] = qv_f[...].astype(BF)
 
-    @pl.loop(1, NS)
-    def _(k):
-        o = (s + k) % NS
-        wait_in(emb_l.at[o], emb_rs.at[o])
+    def score(i):
+        xx = (x + NX - i) % NX
+
+        @pl.loop(0, NZ)
+        def _(k):
+            o = xx * NZ + (z + NZ + NZ - 1 - k) % NZ
+
+            @pl.when(o != s)
+            def _():
+                wait_in(answer.at[o], row_rs.at[o])
+
+        got = answer[pl.ds(xx * NZ, NZ)].reshape(NZ * CAP, D)
+        s_v[:, pl.ds(pl.multiple_of(xx * NZ * CAP, NZ * CAP), NZ * CAP)] = lax.dot_general(
+            qv_v[...], got, nt, preferred_element_type=F32
+        )
+
+    pl.loop(0, NX - 1)(score)
+
+    @pl.loop(1, NX)
+    def _(k):
+        xx = (x + k) % NX
+        wait_in(emb_l.at[pl.ds(xx * NZ, NZ)], line_rs.at[xx])
 
     pieces = emb_l[...].reshape(NS * 32, 128)
     to_passage, from_piece = iota((128, NS * 32), 0), iota((128, NS * 32), 1)
@@ -246,28 +306,11 @@
             pick.astype(F32).astype(BF), pieces, preferred_element_type=F32
         ).astype(BF)
 
-    nt = (((1,), (1,)), ((), ()))
     in_logits = (
         lax.dot_general(qv_v[...], e_v[...], nt, preferred_element_type=F32) / logit_divisor
     )
 
-    @pl.loop(0, NX)
-    def _(i):
-        xx = (x + 2 * NX - 1 - i) % NX
-
-        @pl.loop(0, NZ)
-        def _(k):
-            o = xx * NZ + (z + NZ + NZ - 1 - k) % NZ
-
-            @pl.when(o != s)
-            def _():
-                wait_in(answer.at[o], row_rs.at[o])
-
-        got = answer[pl.ds(xx * NZ, NZ)].reshape(NZ * CAP, D)
-        s_v[:, pl.ds(pl.multiple_of(xx * NZ * CAP, NZ * CAP), NZ * CAP)] = lax.dot_general(
-            qv_v[...], got, nt, preferred_element_type=F32
-        )
-
+    score(NX - 1)
     named = mask_v[...] > 0.5
     neg_logits = jnp.where(named, s_v[...] / logit_divisor, -jnp.inf)
     top = jnp.maximum(
@@ -301,9 +344,7 @@
         xx = (x + 1 + i) % NX
         wait_in(ex_l.at[i], ex_rs.at[i])
         both = own_v[i % 2] + ex_l[i].astype(F32)
-        both = both.reshape(NZ, 2, 16, D // 2)
-        part_a = both[:, 0].reshape(NZ * 16, D // 2)
-        part_b = both[:, 1].reshape(NZ * 16, D // 2)
+        part_a, part_b = both[:RA], both[RA:]
         acc_b[xx] = part_b
         b_s[xx] = part_b.astype(BF)
         for k in range(NY):
@@ -369,6 +410,30 @@
         yy = (y + k) % NY
         remote(b2_s.at[yy], b2_l.at[k - 1], b2_ss.at[k - 1], b2_rs.at[k - 1], yy * NC + c, s).start()
 
+    @pl.loop(1, NS)
+    def _(k):
+        o = (s + k) % NS
+        wait_out(req_s.at[o], req_ss.at[o])
+        wait_out(found.at[o], row_ss.at[o])
+
+    @pl.loop(1, NZ)
+    def _(k):
+        wait_out(emb_s, emb_ss.at[k])
+
+    @pl.loop(1, NX)
+    def _(k):
+        wait_out(emb_l.at[pl.ds(0, NZ)], line_ss.at[k])
+
+    for buf, ss, fs in ((wp_v, wp_ss, fp_ss), (ww_v, ww_ss, fw_ss)):
+
+        @pl.loop(0, NY)
+        def _(k):
+            wait_out(buf.at[g], ss.at[k])
+
+        @pl.loop(1, NY)
+        def _(k):
+            wait_out(buf.at[((y + k) % NY) * NC + c], fs.at[k])
+
     part_a = a2_o[...]
     for k in range(NX - 1):
         wait_in(a2_l.at[k], a2_rs.at[k])
@@ -377,29 +442,51 @@
     for k in range(NY - 1):
         wait_in(b2_l.at[k], b2_rs.at[k])
         part_b = part_b + b2_l[k].astype(F32)
-    part_a = part_a.reshape(NZ, 16, 128)
-    part_b = part_b.reshape(NZ, 16, 128)
-    z_o[:, 0:16, :] = part_a
-    z_o[:, 16:32, :] = part_b
-    z_s[...] = z_o[...].astype(BF)
+    part_a = part_a.reshape(RA // 32, 32, 128)
+    part_b = part_b.reshape(RB // 32, 32, 128)
+    z_o[: RA // 32] = part_a
+    z_o[RA // 32 :] = part_b
+    z_s[: RA // 32] = part_a.astype(BF)
+    z_s[RA // 32 :] = part_b.astype(BF)
 
     @pl.loop(1, NZ)
     def _(k):
         zz = (z + k) % NZ
         remote(z_s.at[zz], z_l.at[k - 1], z_ss.at[k - 1], z_rs.at[k - 1], g, x * NZ + zz).start()
+
+    @pl.loop(0, NX)
+    def _(i):
+        wait_out(ex_s.at[i], ex_ss.at[i])
+
+        @pl.loop(0, NY - 1)
+        def _(k):
+            wait_out(a_s.at[0, 0], a_ss.at[k, i])
+
+    @pl.loop(0, NX - 1)
+    def _(i):
+        wait_out(b_s.at[i], b_ss.at[i])
+        wait_out(a2_s.at[i], a2_ss.at[i])
+
+    @pl.loop(0, NY - 1)
+    def _(i):
+        wait_out(b2_s.at[i], b2_ss.at[i])
 
     total_part = z_o[z]
     for k in range(NZ - 1):
         wait_in(z_l.at[k], z_rs.at[k])
         total_part = total_part + z_l[k].astype(F32)
 
-    f_s[...] = total_part
-    f_l[g] = total_part
+    f_s[...] = total_part.astype(BF)
+    f_l[g] = total_part.astype(BF)
 
     @pl.loop(1, NG)
     def _(k):
         gg = (g + k) % NG
         remote(f_s, f_l.at[g], f_ss.at[k], f_rs.at[g], gg, s).start()
+
+    @pl.loop(0, NZ - 1)
+    def _(i):
+        wait_out(z_s.at[i], z_ss.at[i])
 
     @pl.loop(1, NG)
     def _(k):
@@ -409,59 +496,30 @@
     for yy in range(NY):
         for cc in range(NC):
             at = (cc * NY + yy) * 128
-            grad_ref[:, at : at + 128] = f_l[yy * NC + cc]
-
-    @pl.loop(1, NS)
-    def _(k):
-        o = (s + k) % NS
-        wait_out(req_s.at[o], req_ss.at[o])
-        wait_out(found.at[o], row_ss.at[o])
-        wait_out(emb_s, emb_ss.at[o])
-
-    for buf, ss, fs in ((wp_v, wp_ss, fp_ss), (ww_v, ww_ss, fw_ss)):
-
-        @pl.loop(0, NY)
-        def _(k):
-            wait_out(buf.at[g], ss.at[k])
-
-        @pl.loop(1, NY)
-        def _(k):
-            wait_out(buf.at[((y + k) % NY) * NC + c], fs.at[k])
-
-    @pl.loop(0, NX)
-    def _(i):
-        wait_out(ex_s.at[i], ex_ss.at[i])
-
-        @pl.loop(0, NY - 1)
-        def _(k):
-            wait_out(a_s.at[0, 0], a_ss.at[k, i])
-
-    @pl.loop(0, NX - 1)
-    def _(i):
-        wait_out(b_s.at[i], b_ss.at[i])
-        wait_out(a2_s.at[i], a2_ss.at[i])
-
-    @pl.loop(0, NY - 1)
-    def _(i):
-        wait_out(b2_s.at[i], b2_ss.at[i])
-
-    @pl.loop(0, NZ - 1)
-    def _(i):
-        wait_out(z_s.at[i], z_ss.at[i])
+            grad_ref[:, at : at + 128] = f_l[yy * NC + cc].astype(F32)
 
     @pl.loop(1, NG)
     def _(k):
         wait_out(f_s, f_ss.at[k])
+
+
+def hand_over(grad, loss, emb, grad_out, loss_out, emb_out):
+    grad_out[...] = grad[...]
+    loss_out[...] = loss[...]
+    emb_out[...] = emb[...]
 
 
 def shards(
     query_states, passage_states, index_rows, weight, prev_weight, neg_owner, neg_row, positive
 ):
     vmem = pl.BlockSpec(memory_space=pltpu.VMEM)
-    hbm = pl.BlockSpec(memory_space=pl.ANY)
+    hbm = pl.BlockSpec(memory_space=pltpu.HBM)
     dma = pltpu.SemaphoreType.DMA
     half = D // 2
     scratch = [
+        pltpu.VMEM((NEG, 1, QD), jnp.int32),
+        pltpu.VMEM((NEG, QD), jnp.int32),
+        pltpu.VMEM((1, QD), jnp.int32),
         pltpu.VMEM((TOK, D), BF),
         pltpu.VMEM((D, TOK), BF),
         pltpu.VMEM((PD * PL, D), BF),
@@ -486,30 +544,31 @@
         pltpu.VMEM((NX, 256, half), BF),
         pltpu.VMEM((NX, 256, half), BF),
         pltpu.VMEM((2, 256, half), F32),
-        pltpu.VMEM((NY, NX, 128, 128), F32),
-        pltpu.VMEM((NX, 128, half), F32),
-        pltpu.VMEM((NY, NX, 128, 128), BF),
-        pltpu.VMEM((NX, 128, half), BF),
-        pltpu.VMEM((NY - 1, NX, 128, 128), BF),
-        pltpu.VMEM((NX - 1, 128, half), BF),
-        pltpu.VMEM((NX - 1, 128, 128), BF),
-        pltpu.VMEM((NY, 128, 128), BF),
-        pltpu.VMEM((NX - 1, 128, 128), BF),
-        pltpu.VMEM((NY - 1, 128, 128), BF),
-        pltpu.VMEM((128, 128), F32),
-        pltpu.VMEM((NY, 128, 128), F32),
+        pltpu.VMEM((NY, NX, RA, 128), F32),
+        pltpu.VMEM((NX, RB, half), F32),
+        pltpu.VMEM((NY, NX, RA, 128), BF),
+        pltpu.VMEM((NX, RB, half), BF),
+        pltpu.VMEM((NY - 1, NX, RA, 128), BF),
+        pltpu.VMEM((NX - 1, RB, half), BF),
+        pltpu.VMEM((NX - 1, RA, 128), BF),
+        pltpu.VMEM((NY, RB, 128), BF),
+        pltpu.VMEM((NX - 1, RA, 128), BF),
+        pltpu.VMEM((NY - 1, RB, 128), BF),
+        pltpu.VMEM((RA, 128), F32),
+        pltpu.VMEM((NY, RB, 128), F32),
         pltpu.VMEM((NZ, 32, 128), BF),
         pltpu.VMEM((NZ - 1, 32, 128), BF),
         pltpu.VMEM((NZ, 32, 128), F32),
-        pltpu.VMEM((32, 128), F32),
-        pltpu.VMEM((NG, 32, 128), F32),
-        dma((5,)),
+        pltpu.VMEM((32, 128), BF),
+        pltpu.VMEM((NG, 32, 128), BF),
+        dma((8,)),
         dma((NS,)), dma((NS,)),
         dma((NS,)), dma((NS,)),
         dma((NY,)), dma((NG,)),
         dma((NY,)), dma((NG,)),
         dma((NY,)), dma((NY,)),
-        dma((NS,)), dma((NS,)),
+        dma((NZ,)), dma((NZ,)),
+        dma((NX,)), dma((NX,)),
         dma((NX,)), dma((NX,)),
         dma((NY - 1, NX)), dma((NY - 1, NX)),
         dma((NX - 1,)), dma((NX - 1,)),
@@ -525,7 +584,7 @@
             jax.ShapeDtypeStruct((1, QD), F32),
             jax.ShapeDtypeStruct((PD, D), BF),
         ),
-        in_specs=[vmem] * 3 + [hbm] * 5,
+        in_specs=[hbm] * 8,
         out_specs=(vmem, vmem, vmem),
         scratch_shapes=scratch,
         compiler_params=pltpu.CompilerParams(
@@ -536,8 +595,8 @@
         ),
         name="retriever_step",
     )(
-        neg_owner.reshape(QD, NEG),
-        neg_row,
+        neg_owner.transpose(1, 2, 0),
+        neg_row.T,
         positive.reshape(1, QD),
         query_states.reshape(TOK, D),
         passage_states.reshape(PD * PL, D),
@@ -545,6 +604,17 @@
         weight,
         prev_weight,
     )
+    grad, loss, emb = pl.pallas_call(
+        hand_over,
+        out_shape=(
+            jax.ShapeDtypeStruct((D // NS, D), F32),
+            jax.ShapeDtypeStruct((1, QD), F32),
+            jax.ShapeDtypeStruct((PD, D), BF),
+        ),
+        in_specs=[vmem] * 3,
+        out_specs=(vmem, vmem, vmem),
+        name="hand_over",
+    )(grad, loss, emb)
     return grad, loss.reshape(QD), emb
 
 

time: 112 us -> 98.7 us (0.88)
  Pallas kernels: 105 us -> 98 us
  local copies, waits for them, and re-layouts: 6.8 us -> 0 us
    pallas_call x1, Pallas kernels: 105 us -> 96.4 us  [shards(): pl.pallas_call(kernel, out_shape=(jax.ShapeDtypeStruct((D // NS, D), F32)...]
    unnamed x5 -> x0, local copies, waits for them, and re-layouts: 6.8 us -> none
    pallas_call x0 -> x1, Pallas kernels: none -> 1.58 us  [shards(): pl.pallas_call(hand_over, out_shape=(jax.ShapeDtypeStruct((D // NS, D), F...]
where the time goes in v2:
time: 98.7 us; the launch traced here: 98.6 us
  Pallas kernels  98 us (99%)
    pallas_call x1, Pallas kernels, shards(): pl.pallas_call(kernel, out_shape=(jax.ShapeDtypeStruct((D // NS, D), F32)...  96.4 us

profile of v2, /device:TPU:1, one launch (start us, length us, event | category | flops | bytes accessed | tf_op | source)
XLA Modules:
  0.0 98.6 jit_solution(15169842339645843918)
XLA Ops:
  0.6 96.4 %retriever_step.1 = (f32[32,1024]{1,0:T(8,128)}, f32[1,64]{1,0:T(1,128)}, bf16[4,1024]{1,0:T(4,128)(2,1)}) custom-call(s32[8,1,64]{2,1,0:T(1,128)} %bitcast.8, s32[8,64]{1,0:T(8,128)} %bitcast.9, s32[1,64]{1,0:T(1,128)} %bitcast.10, bf16[2048,1024]{1,0:T(8,128)(2,1)} %bitcast.6, bf16[512,1024]{1,0:T(8,128)(2,1)} %bitcast.7, bf16[2048,1024]{1,0:T(8,128)(2,1)} %idx_hbm.1, ...), custom_call_target="tpu_custom_call" | custom-call | flops 17179869184 | bytes 12582912 | tf_op jit(solution)/shard_map/retriever_step/pallas_call | solution.py:580
  97.0 1.6 %hand_over.1 = (f32[32,1024]{1,0:T(8,128)}, f32[1,64]{1,0:T(1,128)}, bf16[4,1024]{1,0:T(4,128)(2,1)}) custom-call(f32[32,1024]{1,0:T(8,128)} %get-tuple-element.9.grad, f32[1,64]{1,0:T(1,128)} %get-tuple-element.10.loss, bf16[4,1024]{1,0:T(4,128)(2,1)} %get-tuple-element.11.emb), custom_call_target="tpu_custom_call" | custom-call | tf_op jit(solution)/shard_map/hand_over/pallas_call | solution.py:607

commit v3 on v2

--- a/solution.py
+++ b/solution.py
@@ -26,7 +26,8 @@
 NG, NS = NY * NC, NX * NZ
 TOK = QD * QL
 SLOTS = NS * CAP
-RA, RB = 5 * 32, 3 * 32
+ZA, ZB = 5, 3
+RA, RB = ZA * 32, ZB * 32
 GRAD_SCALE = 1.0 / (logit_divisor * math.sqrt(QD * NS * NG))
 
 
@@ -52,10 +53,10 @@
     emb_f, emb_s, emb_l, e_v,
     d1_v, qv_f, qv_v, s_v, qg_v, hg_v,
     ex_s, ex_l, own_v, acc_a, acc_b, a_s, b_s, a_l, b_l,
-    a2_s, b2_s, a2_l, b2_l, a2_o, b2_o, z_s, z_l, z_o, f_s, f_l,
+    za_s, zb_s, za_o, zb_o, z_l, f_s, f_l,
     loc_sem, req_ss, req_rs, row_ss, row_rs, wp_ss, wp_rs, ww_ss, ww_rs,
     fp_ss, fw_ss, emb_ss, emb_rs, line_ss, line_rs, ex_ss, ex_rs, a_ss, a_rs, b_ss, b_rs,
-    a2_ss, a2_rs, b2_ss, b2_rs, z_ss, z_rs, f_ss, f_rs,
+    za_ss, zb_ss, z_rs, f_ss, f_rs,
 ):
     g, s = lax.axis_index("group"), lax.axis_index("shard")
     y, c = g // NC, g % NC
@@ -96,6 +97,13 @@
     @pl.loop(1, NG)
     def _(k):
         pl.semaphore_signal(barrier, inc=1, device_id=((g + k) % NG, s), device_id_type=MESH)
+
+    @pl.loop(1, NY)
+    def _(k):
+        @pl.loop(1, NZ)
+        def _(j):
+            peer = ((y + k) % NY * NC + c, x * NZ + (z + j) % NZ)
+            pl.semaphore_signal(barrier, inc=1, device_id=peer, device_id_type=MESH)
 
     local_copies = [
         local(idx_hbm, idx_v, 0),
@@ -132,11 +140,11 @@
     for o in range(NS):
         req_s[o] = requests[o : o + 1, :]
 
-    pl.semaphore_wait(barrier, NS - 1 + NG - 1)
+    pl.semaphore_wait(barrier, NS - 1 + NG - 1 + (NY - 1) * (NZ - 1))
 
     @pl.loop(1, NS)
     def _(k):
-        o = (s + k) % NS
+        o = (x + k // NZ) % NX * NZ + (z + k) % NZ
         remote(req_s.at[o], req_l.at[s], req_ss.at[o], req_rs.at[s], g, o).start()
 
     req_l[s] = req_s[s]
@@ -153,44 +161,47 @@
     local_copies[0].wait()
     row_lane = iota((128, ROWS), 1)
 
-    def send_rows(i):
-        xx = (x + i) % NX
-
-        @pl.loop(0, NZ)
-        def _(k):
-            r = xx * NZ + (z + 1 + k) % NZ
-
-            @pl.when(r != s)
+    sets = ((4, 1, 2, 7), (0, 5, 6, 3))
+
+    def send_rows(i, half):
+        for step in sets[half]:
+            r = (x + i) % NX * NZ + (z + step) % NZ
+
+            def send():
+                remote(
+                    found.at[i, half, r % 4], answer.at[s], row_ss.at[r], row_rs.at[s], g, r
+                ).start()
+
+            if step:
+                send()
+            else:
+                pl.when(i > 0)(send)
+
+    @pl.loop(0, NX)
+    def _(i):
+        for half in range(2):
+            ids = jnp.zeros((1, 128), F32)
+            for step in sets[half]:
+                r = (x + i) % NX * NZ + (z + step) % NZ
+
+                def wait():
+                    wait_in(req_l.at[r], req_rs.at[r])
+
+                if step:
+                    wait()
+                else:
+                    pl.when(i > 0)(wait)
+                ids = ids + req_l[r]
+            column = to_column(ids, 128).astype(jnp.int32)
+            hot = (row_lane == column).astype(F32).astype(BF)
+            got = jnp.dot(hot, idx_v[...], preferred_element_type=F32).astype(BF)
+            found[i, half] = got.reshape(4, CAP, D)
+
+            @pl.when(i < NX // 2)
             def _():
-                remote(found.at[r], answer.at[s], row_ss.at[r], row_rs.at[s], g, r).start()
-
-    @pl.loop(0, NX)
-    def _(i):
-        xx = (x + i) % NX
-
-        @pl.loop(0, NZ)
-        def _(k):
-            r = xx * NZ + (z + 1 + k) % NZ
-
-            @pl.when(r != s)
-            def _():
-                wait_in(req_l.at[r], req_rs.at[r])
-
-        hots = []
-        for half in range(NZ // 4):
-            first = xx * NZ + half * 4
-            ids = req_l[first] + req_l[first + 1] + req_l[first + 2] + req_l[first + 3]
-            column = to_column(ids, 128).astype(jnp.int32)
-            hots.append((row_lane == column).astype(F32).astype(BF))
-        hot = jnp.concatenate(hots, axis=0)
-        got = jnp.dot(hot, idx_v[...], preferred_element_type=F32).astype(BF)
-        found[pl.ds(xx * NZ, NZ)] = got.reshape(NZ, CAP, D)
-
-        @pl.when(i < NX // 2)
-        def _():
-            send_rows(i)
-
-    answer[s] = found[s]
+                send_rows(i, half)
+
+    answer[s] = found[0, 1, s % 4]
 
     slot_lane = iota((QD, SLOTS), 1)
     mask = jnp.zeros((QD, SLOTS), F32)
@@ -244,7 +255,8 @@
         zz = (z + k) % NZ
         remote(emb_s, emb_l.at[s], emb_ss.at[k], emb_rs.at[z], g, x * NZ + zz).start()
 
-    send_rows(2)
+    send_rows(2, 0)
+    send_rows(2, 1)
 
     local_copies[2].wait()
     gather_rest(ww_v, ww_rs, fw_ss)
@@ -261,7 +273,8 @@
         xx = (x + k) % NX
         remote(line, line, line_ss.at[k], line_rs.at[x], g, xx * NZ + z).start()
 
-    send_rows(3)
+    send_rows(3, 0)
+    send_rows(3, 1)
 
     @pl.loop(0, TOK // 256)
     def _(i):
@@ -379,42 +392,62 @@
 
     finish(NX - 1)
 
-    @pl.loop(0, NX)
-    def _(i):
+    def second_a(i):
         xx = (x + 1 + i) % NX
         part = acc_a[y, xx]
         for k in range(1, NY):
             wait_in(a_l.at[k - 1, xx], a_rs.at[k - 1, i])
             part = part + a_l[k - 1, xx].astype(F32)
-
-        @pl.when(i < NX - 1)
-        def _():
-            a2_s[i] = part.astype(BF)
-            remote(a2_s.at[i], a2_l.at[i], a2_ss.at[i], a2_rs.at[i], g, xx * NZ + z).start()
+        part = part.reshape(ZA, 32, 128)
+        za_s[xx] = part.astype(BF)
 
         @pl.when(i == NX - 1)
         def _():
-            a2_o[...] = part
+            za_o[...] = part
+
+        @pl.loop(0, NZ)
+        def _(k):
+            zz = (z + 1 + k) % NZ
+
+            @pl.when(zz < ZA)
+            def _():
+                @pl.when(xx * NZ + zz != s)
+                def _():
+                    remote(
+                        za_s.at[xx, zz], z_l.at[s], za_ss.at[xx, zz], z_rs.at[s], g, xx * NZ + zz
+                    ).start()
+
+    pl.loop(0, NX - 1)(second_a)
 
     part_b = acc_b[x]
     for k in range(NX - 1):
         wait_in(b_l.at[k], b_rs.at[k])
         part_b = part_b + b_l[k].astype(F32)
     for k in range(NY):
-        piece = part_b[:, k * 128 : (k + 1) * 128]
-        b2_o[k] = piece
-        b2_s[k] = piece.astype(BF)
-
-    @pl.loop(1, NY)
-    def _(k):
-        yy = (y + k) % NY
-        remote(b2_s.at[yy], b2_l.at[k - 1], b2_ss.at[k - 1], b2_rs.at[k - 1], yy * NC + c, s).start()
+        piece = part_b[:, k * 128 : (k + 1) * 128].reshape(ZB, 32, 128)
+        zb_o[k] = piece
+        zb_s[k] = piece.astype(BF)
+
+    @pl.loop(0, NY)
+    def _(k):
+        yy = (y + 1 + k) % NY
+
+        @pl.loop(0, ZB)
+        def _(j):
+            @pl.when((yy - y) * NZ + ZA + j - z != 0)
+            def _():
+                remote(
+                    zb_s.at[yy, j], z_l.at[y * NZ + z], zb_ss.at[yy, j], z_rs.at[y * NZ + z],
+                    yy * NC + c, x * NZ + ZA + j,
+                ).start()
+
+    second_a(NX - 1)
 
     @pl.loop(1, NS)
     def _(k):
         o = (s + k) % NS
         wait_out(req_s.at[o], req_ss.at[o])
-        wait_out(found.at[o], row_ss.at[o])
+        wait_out(found.at[0, 0, 0], row_ss.at[o])
 
     @pl.loop(1, NZ)
     def _(k):
@@ -434,26 +467,6 @@
         def _(k):
             wait_out(buf.at[((y + k) % NY) * NC + c], fs.at[k])
 
-    part_a = a2_o[...]
-    for k in range(NX - 1):
-        wait_in(a2_l.at[k], a2_rs.at[k])
-        part_a = part_a + a2_l[k].astype(F32)
-    part_b = b2_o[y]
-    for k in range(NY - 1):
-        wait_in(b2_l.at[k], b2_rs.at[k])
-        part_b = part_b + b2_l[k].astype(F32)
-    part_a = part_a.reshape(RA // 32, 32, 128)
-    part_b = part_b.reshape(RB // 32, 32, 128)
-    z_o[: RA // 32] = part_a
-    z_o[RA // 32 :] = part_b
-    z_s[: RA // 32] = part_a.astype(BF)
-    z_s[RA // 32 :] = part_b.astype(BF)
-
-    @pl.loop(1, NZ)
-    def _(k):
-        zz = (z + k) % NZ
-        remote(z_s.at[zz], z_l.at[k - 1], z_ss.at[k - 1], z_rs.at[k - 1], g, x * NZ + zz).start()
-
     @pl.loop(0, NX)
     def _(i):
         wait_out(ex_s.at[i], ex_ss.at[i])
@@ -465,38 +478,52 @@
     @pl.loop(0, NX - 1)
     def _(i):
         wait_out(b_s.at[i], b_ss.at[i])
-        wait_out(a2_s.at[i], a2_ss.at[i])
-
-    @pl.loop(0, NY - 1)
-    def _(i):
-        wait_out(b2_s.at[i], b2_ss.at[i])
-
-    total_part = z_o[z]
-    for k in range(NZ - 1):
-        wait_in(z_l.at[k], z_rs.at[k])
-        total_part = total_part + z_l[k].astype(F32)
-
-    f_s[...] = total_part.astype(BF)
-    f_l[g] = total_part.astype(BF)
+
+    def collect(me, own):
+        @pl.loop(1, NS)
+        def _(k):
+            wait_in(z_l.at[(me + k) % NS], z_rs.at[(me + k) % NS])
+
+        total_part = own
+        for k in range(1, NS):
+            total_part = total_part + z_l[(me + k) % NS].astype(F32)
+        f_s[...] = total_part.astype(BF)
+
+    @pl.when(z < ZA)
+    def _():
+        collect(x * NZ + z, za_o[z])
+
+    @pl.when(z >= ZA)
+    def _():
+        collect(y * NZ + z, zb_o[y, z - ZA])
+
+    f_l[g] = f_s[...]
 
     @pl.loop(1, NG)
     def _(k):
         gg = (g + k) % NG
         remote(f_s, f_l.at[g], f_ss.at[k], f_rs.at[g], gg, s).start()
 
-    @pl.loop(0, NZ - 1)
-    def _(i):
-        wait_out(z_s.at[i], z_ss.at[i])
+    @pl.loop(0, NX)
+    def _(i):
+        @pl.loop(0, ZA)
+        def _(k):
+            @pl.when((i - x) * NZ + k - z != 0)
+            def _():
+                wait_out(za_s.at[i, k], za_ss.at[i, k])
+
+        @pl.loop(0, ZB)
+        def _(k):
+            @pl.when((i - y) * NZ + ZA + k - z != 0)
+            def _():
+                wait_out(zb_s.at[i, k], zb_ss.at[i, k])
 
     @pl.loop(1, NG)
     def _(k):
         gg = (g + k) % NG
         wait_in(f_l.at[gg], f_rs.at[gg])
 
-    for yy in range(NY):
-        for cc in range(NC):
-            at = (cc * NY + yy) * 128
-            grad_ref[:, at : at + 128] = f_l[yy * NC + cc].astype(F32)
+    grad_ref[...] = f_l[...]
 
     @pl.loop(1, NG)
     def _(k):
@@ -504,7 +531,10 @@
 
 
 def hand_over(grad, loss, emb, grad_out, loss_out, emb_out):
-    grad_out[...] = grad[...]
+    for y in range(NY):
+        for c in range(NC):
+            at = (c * NY + y) * 128
+            grad_out[:, at : at + 128] = grad[y * NC + c].astype(F32)
     loss_out[...] = loss[...]
     emb_out[...] = emb[...]
 
@@ -528,7 +558,7 @@
         pltpu.VMEM((NG, D // NG, D), BF),
         pltpu.VMEM((NS, 1, 128), F32),
         pltpu.VMEM((NS, 1, 128), F32),
-        pltpu.VMEM((NS, CAP, D), BF),
+        pltpu.VMEM((NX, 2, 4, CAP, D), BF),
         pltpu.VMEM((NS, CAP, D), BF),
         pltpu.VMEM((QD, SLOTS), F32),
         pltpu.VMEM((32, 128), F32),
@@ -550,15 +580,11 @@
         pltpu.VMEM((NX, RB, half), BF),
         pltpu.VMEM((NY - 1, NX, RA, 128), BF),
         pltpu.VMEM((NX - 1, RB, half), BF),
-        pltpu.VMEM((NX - 1, RA, 128), BF),
-        pltpu.VMEM((NY, RB, 128), BF),
-        pltpu.VMEM((NX - 1, RA, 128), BF),
-        pltpu.VMEM((NY - 1, RB, 128), BF),
-        pltpu.VMEM((RA, 128), F32),
-        pltpu.VMEM((NY, RB, 128), F32),
-        pltpu.VMEM((NZ, 32, 128), BF),
-        pltpu.VMEM((NZ - 1, 32, 128), BF),
-        pltpu.VMEM((NZ, 32, 128), F32),
+        pltpu.VMEM((NX, ZA, 32, 128), BF),
+        pltpu.VMEM((NY, ZB, 32, 128), BF),
+        pltpu.VMEM((ZA, 32, 128), F32),
+        pltpu.VMEM((NY, ZB, 32, 128), F32),
+        pltpu.VMEM((NS, 32, 128), BF),
         pltpu.VMEM((32, 128), BF),
         pltpu.VMEM((NG, 32, 128), BF),
         dma((8,)),
@@ -572,15 +598,13 @@
         dma((NX,)), dma((NX,)),
         dma((NY - 1, NX)), dma((NY - 1, NX)),
         dma((NX - 1,)), dma((NX - 1,)),
-        dma((NX - 1,)), dma((NX - 1,)),
-        dma((NY - 1,)), dma((NY - 1,)),
-        dma((NZ - 1,)), dma((NZ - 1,)),
+        dma((NX, ZA)), dma((NY, ZB)), dma((NS,)),
         dma((NG,)), dma((NG,)),
     ]
     grad, loss, emb = pl.pallas_call(
         kernel,
         out_shape=(
-            jax.ShapeDtypeStruct((D // NS, D), F32),
+            jax.ShapeDtypeStruct((NG, 32, 128), BF),
             jax.ShapeDtypeStruct((1, QD), F32),
             jax.ShapeDtypeStruct((PD, D), BF),
         ),

time: 98.7 us -> 95.6 us (0.969)
  Pallas kernels: 98 us -> 94.9 us
    pallas_call x1, Pallas kernels: 96.4 us -> 93.3 us  [shards(): pl.pallas_call(kernel, out_shape=(jax.ShapeDtypeStruct((NG, 32, 128), BF)...]
where the time goes in v3:
time: 95.6 us; the launch traced here: 95.5 us
  Pallas kernels  94.9 us (99%)
    pallas_call x1, Pallas kernels, shards(): pl.pallas_call(kernel, out_shape=(jax.ShapeDtypeStruct((NG, 32, 128), BF)...  93.3 us

profile of v3, /device:TPU:1, one launch (start us, length us, event | category | flops | bytes accessed | tf_op | source)
XLA Modules:
  0.0 95.5 jit_solution(11384383620479115083)
XLA Ops:
  0.6 93.3 %retriever_step.1 = (bf16[8,32,128]{2,1,0:T(8,128)(2,1)}, f32[1,64]{1,0:T(1,128)}, bf16[4,1024]{1,0:T(4,128)(2,1)}) custom-call(s32[8,1,64]{2,1,0:T(1,128)} %bitcast.8, s32[8,64]{1,0:T(8,128)} %bitcast.9, s32[1,64]{1,0:T(1,128)} %bitcast.10, bf16[2048,1024]{1,0:T(8,128)(2,1)} %bitcast.6, bf16[512,1024]{1,0:T(8,128)(2,1)} %bitcast.7, ...), custom_call_target="tpu_custom_call" | custom-call | flops 17179869184 | bytes 12582912 | tf_op jit(solution)/shard_map/retriever_step/pallas_call | solution.py:604
  94.0 1.5 %hand_over.1 = (f32[32,1024]{1,0:T(8,128)}, f32[1,64]{1,0:T(1,128)}, bf16[4,1024]{1,0:T(4,128)(2,1)}) custom-call(bf16[8,32,128]{2,1,0:T(8,128)(2,1)} %get-tuple-element.9.grad, f32[1,64]{1,0:T(1,128)} %get-tuple-element.10.loss, bf16[4,1024]{1,0:T(4,128)(2,1)} %get-tuple-element.11.emb), custom_call_target="tpu_custom_call" | custom-call | tf_op jit(solution)/shard_map/hand_over/pallas_call | solution.py:631

commit v4 on v3

--- a/solution.py
+++ b/solution.py
@@ -26,7 +26,7 @@
 NG, NS = NY * NC, NX * NZ
 TOK = QD * QL
 SLOTS = NS * CAP
-ZA, ZB = 5, 3
+ZA, ZB = 4, 4
 RA, RB = ZA * 32, ZB * 32
 GRAD_SCALE = 1.0 / (logit_divisor * math.sqrt(QD * NS * NG))
 
@@ -47,8 +47,8 @@
 
 def kernel(
     owner_hbm, row_hbm, pos_hbm, x_hbm, p_hbm, idx_hbm, w_hbm, pw_hbm,
-    grad_ref, loss_ref, emb_ref,
-    owner_ref, row_ref, pos_ref, x_v, xt_v, p_v, idx_v, wp_v, ww_v,
+    grad_hbm, loss_hbm, emb_hbm,
+    owner_ref, row_ref, pos_ref, loss_v, x_v, xt_v, p_v, idx_v, wp_v, ww_v,
     req_s, req_l, found, answer, mask_v,
     emb_f, emb_s, emb_l, e_v,
     d1_v, qv_f, qv_v, s_v, qg_v, hg_v,
@@ -149,7 +149,7 @@
 
     req_l[s] = req_s[s]
 
-    for hbm, buf, ss, rs in ((pw_hbm, wp_v, wp_ss, wp_rs), (w_hbm, ww_v, ww_ss, ww_rs)):
+    def spread(hbm, buf, ss, rs):
 
         @pl.loop(1, NY)
         def _(k):
@@ -157,6 +157,8 @@
             remote(hbm, buf.at[g], ss.at[k], rs.at[g], peer, s).start()
 
         remote(hbm, buf.at[g], ss.at[0], rs.at[g], sib, s).start()
+
+    spread(pw_hbm, wp_v, wp_ss, wp_rs)
 
     local_copies[0].wait()
     row_lane = iota((128, ROWS), 1)
@@ -202,6 +204,7 @@
                 send_rows(i, half)
 
     answer[s] = found[0, 1, s % 4]
+    spread(w_hbm, ww_v, ww_ss, ww_rs)
 
     slot_lane = iota((QD, SLOTS), 1)
     mask = jnp.zeros((QD, SLOTS), F32)
@@ -247,8 +250,7 @@
     emb = emb_f[...].astype(BF)
     emb_s[...] = emb
     emb_l[s] = emb
-    for b in range(8):
-        emb_ref[:, b * 128 : (b + 1) * 128] = emb_f[b * PD : (b + 1) * PD, :].astype(BF)
+    local(emb_s, emb_hbm, 8).start()
 
     @pl.loop(1, NZ)
     def _(k):
@@ -335,7 +337,8 @@
     label = (iota((QD, 128), 1) == to_column(pos_ref[...].astype(F32), QD).astype(jnp.int32))
     label = label.astype(F32)
     picked = jnp.sum(in_logits * label, axis=1, keepdims=True)
-    loss_ref[...] = to_row(jnp.log(total) + top - picked, QD)
+    loss_v[...] = to_row(jnp.log(total) + top - picked, QD)
+    local(loss_v, loss_hbm, 9).start()
     coeff_in = (in_exp / total - label).astype(BF)
     coeff_neg = (neg_exp / total).astype(BF)
     query_grad = jnp.dot(coeff_in, e_v[...], preferred_element_type=F32) + jnp.dot(
@@ -343,18 +346,23 @@
     )
     qg_v[...] = query_grad * GRAD_SCALE * (1.0 / QL)
 
-    @pl.loop(0, QD // 8)
-    def _(i):
-        q_at = pl.multiple_of(i * 8, 8)
-        grads = qg_v[pl.ds(q_at, 8), :]
-        for j in range(8):
-            at = pl.multiple_of(i * 256 + j * QL, QL)
-            value = (d1_v[pl.ds(at, QL), :] * grads[j : j + 1, :]).astype(BF)
-            hg_v[0, pl.ds(at, QL), :] = value[:, : D // 2]
-            hg_v[1, pl.ds(at, QL), :] = value[:, D // 2 :]
+    def gradient_of_hidden(half):
+        columns = pl.ds(pl.multiple_of(half * (D // 2), D // 2), D // 2)
+
+        @pl.loop(0, QD // 8)
+        def _(i):
+            grads = qg_v[pl.ds(pl.multiple_of(i * 8, 8), 8), columns]
+            for j in range(8):
+                at = pl.ds(pl.multiple_of(i * 256 + j * QL, QL), QL)
+                hg_v[half, at, :] = (d1_v[at, columns] * grads[j : j + 1, :]).astype(BF)
+
+    gradient_of_hidden(1 - c)
+
+    def turn(i):
+        return (x + 2 - i + 3 * (i // 2) + 2 * (i // 3)) % NX
 
     def finish(i):
-        xx = (x + 1 + i) % NX
+        xx = turn(i)
         wait_in(ex_l.at[i], ex_rs.at[i])
         both = own_v[i % 2] + ex_l[i].astype(F32)
         part_a, part_b = both[:RA], both[RA:]
@@ -379,11 +387,15 @@
 
     @pl.loop(0, NX)
     def _(i):
-        xx = (x + 1 + i) % NX
+        xx = turn(i)
         left = xt_v[pl.ds(pl.multiple_of(xx * 256, 256), 256), :]
         ex_s[i] = jnp.dot(left, hg_v[1 - c], preferred_element_type=F32).astype(BF)
         remote(ex_s.at[i], ex_l.at[i], ex_ss.at[i], ex_rs.at[i], sib, s).start()
 
+        @pl.when(i == 0)
+        def _():
+            gradient_of_hidden(c)
+
         @pl.when(i > 0)
         def _():
             finish(i - 1)
@@ -392,8 +404,8 @@
 
     finish(NX - 1)
 
-    def second_a(i):
-        xx = (x + 1 + i) % NX
+    def second_a(i, own=False):
+        xx = turn(i)
         part = acc_a[y, xx]
         for k in range(1, NY):
             wait_in(a_l.at[k - 1, xx], a_rs.at[k - 1, i])
@@ -401,23 +413,24 @@
         part = part.reshape(ZA, 32, 128)
         za_s[xx] = part.astype(BF)
 
-        @pl.when(i == NX - 1)
-        def _():
+        if own:
             za_o[...] = part
 
-        @pl.loop(0, NZ)
-        def _(k):
-            zz = (z + 1 + k) % NZ
-
-            @pl.when(zz < ZA)
-            def _():
-                @pl.when(xx * NZ + zz != s)
-                def _():
-                    remote(
-                        za_s.at[xx, zz], z_l.at[s], za_ss.at[xx, zz], z_rs.at[s], g, xx * NZ + zz
-                    ).start()
-
-    pl.loop(0, NX - 1)(second_a)
+        for zz in range(ZA):
+
+            def send():
+                remote(
+                    za_s.at[xx, zz], z_l.at[s], za_ss.at[xx, zz], z_rs.at[s], g, xx * NZ + zz
+                ).start()
+
+            if own:
+                pl.when(zz != z)(send)
+            else:
+                send()
+
+    @pl.loop(0, NX - 1)
+    def _(i):
+        second_a(i)
 
     part_b = acc_b[x]
     for k in range(NX - 1):
@@ -428,20 +441,22 @@
         zb_o[k] = piece
         zb_s[k] = piece.astype(BF)
 
-    @pl.loop(0, NY)
-    def _(k):
+    for k in range(NY):
         yy = (y + 1 + k) % NY
-
-        @pl.loop(0, ZB)
-        def _(j):
-            @pl.when((yy - y) * NZ + ZA + j - z != 0)
-            def _():
+        for j in range(ZB):
+
+            def send():
                 remote(
                     zb_s.at[yy, j], z_l.at[y * NZ + z], zb_ss.at[yy, j], z_rs.at[y * NZ + z],
                     yy * NC + c, x * NZ + ZA + j,
                 ).start()
 
-    second_a(NX - 1)
+            if k == NY - 1:
+                pl.when(z != ZA + j)(send)
+            else:
+                send()
+
+    second_a(NX - 1, own=True)
 
     @pl.loop(1, NS)
     def _(k):
@@ -523,11 +538,15 @@
         gg = (g + k) % NG
         wait_in(f_l.at[gg], f_rs.at[gg])
 
-    grad_ref[...] = f_l[...]
+    local(f_l, grad_hbm, 10).start()
 
     @pl.loop(1, NG)
     def _(k):
         wait_out(f_s, f_ss.at[k])
+
+    local(emb_s, emb_hbm, 8).wait()
+    local(loss_v, loss_hbm, 9).wait()
+    local(f_l, grad_hbm, 10).wait()
 
 
 def hand_over(grad, loss, emb, grad_out, loss_out, emb_out):
@@ -536,7 +555,9 @@
             at = (c * NY + y) * 128
             grad_out[:, at : at + 128] = grad[y * NC + c].astype(F32)
     loss_out[...] = loss[...]
-    emb_out[...] = emb[...]
+    parts = emb[...].astype(F32)
+    for b in range(8):
+        emb_out[:, b * 128 : (b + 1) * 128] = parts[b * PD : (b + 1) * PD, :].astype(BF)
 
 
 def shards(
@@ -550,6 +571,7 @@
         pltpu.VMEM((NEG, 1, QD), jnp.int32),
         pltpu.VMEM((NEG, QD), jnp.int32),
         pltpu.VMEM((1, QD), jnp.int32),
+        pltpu.VMEM((1, QD), F32),
         pltpu.VMEM((TOK, D), BF),
         pltpu.VMEM((D, TOK), BF),
         pltpu.VMEM((PD * PL, D), BF),
@@ -587,7 +609,7 @@
         pltpu.VMEM((NS, 32, 128), BF),
         pltpu.VMEM((32, 128), BF),
         pltpu.VMEM((NG, 32, 128), BF),
-        dma((8,)),
+        dma((11,)),
         dma((NS,)), dma((NS,)),
         dma((NS,)), dma((NS,)),
         dma((NY,)), dma((NG,)),
@@ -606,10 +628,10 @@
         out_shape=(
             jax.ShapeDtypeStruct((NG, 32, 128), BF),
             jax.ShapeDtypeStruct((1, QD), F32),
-            jax.ShapeDtypeStruct((PD, D), BF),
+            jax.ShapeDtypeStruct((PD * 8, 128), BF),
         ),
         in_specs=[hbm] * 8,
-        out_specs=(vmem, vmem, vmem),
+        out_specs=(hbm, hbm, hbm),
         scratch_shapes=scratch,
         compiler_params=pltpu.CompilerParams(
             collective_id=0, has_side_effects=True, vmem_limit_bytes=60 << 20

time: 95.6 us -> 95.5 us (level)
  no operation moved by 1% of the time
where the time goes in v4:
time: 95.5 us; the launch traced here: 95.4 us
  Pallas kernels  94.8 us (99%)
    pallas_call x1, Pallas kernels, shards(): pl.pallas_call(kernel, out_shape=(jax.ShapeDtypeStruct((NG, 32, 128), BF)...  93.3 us

profile of v4, /device:TPU:1, one launch (start us, length us, event | category | flops | bytes accessed | tf_op | source)
XLA Modules:
  0.0 95.4 jit_solution(11670424676935233643)
XLA Ops:
  0.6 93.3 %retriever_step.1 = (bf16[8,32,128]{2,1,0:T(8,128)(2,1)}, f32[1,64]{1,0:T(1,128)}, bf16[32,128]{1,0:T(8,128)(2,1)}) custom-call(s32[8,1,64]{2,1,0:T(1,128)} %bitcast.8, s32[8,64]{1,0:T(8,128)} %bitcast.9, s32[1,64]{1,0:T(1,128)} %bitcast.10, bf16[2048,1024]{1,0:T(8,128)(2,1)} %bitcast.6, bf16[512,1024]{1,0:T(8,128)(2,1)} %bitcast.7, ...), custom_call_target="tpu_custom_call" | custom-call | flops 17179869184 | bytes 12582912 | tf_op jit(solution)/shard_map/retriever_step/pallas_call | solution.py:626
  93.9 1.5 %hand_over.1 = (f32[32,1024]{1,0:T(8,128)}, f32[1,64]{1,0:T(1,128)}, bf16[4,1024]{1,0:T(4,128)(2,1)}) custom-call(bf16[8,32,128]{2,1,0:T(8,128)(2,1)} %get-tuple-element.9.grad, f32[1,64]{1,0:T(1,128)} %get-tuple-element.10.loss, bf16[32,128]{1,0:T(8,128)(2,1)} %get-tuple-element.11.emb), custom_call_target="tpu_custom_call" | custom-call | tf_op jit(solution)/shard_map/hand_over/pallas_call | solution.py:653

commit v5 on v4

--- a/solution.py
+++ b/solution.py
@@ -97,13 +97,6 @@
     @pl.loop(1, NG)
     def _(k):
         pl.semaphore_signal(barrier, inc=1, device_id=((g + k) % NG, s), device_id_type=MESH)
-
-    @pl.loop(1, NY)
-    def _(k):
-        @pl.loop(1, NZ)
-        def _(j):
-            peer = ((y + k) % NY * NC + c, x * NZ + (z + j) % NZ)
-            pl.semaphore_signal(barrier, inc=1, device_id=peer, device_id_type=MESH)
 
     local_copies = [
         local(idx_hbm, idx_v, 0),
@@ -140,7 +133,7 @@
     for o in range(NS):
         req_s[o] = requests[o : o + 1, :]
 
-    pl.semaphore_wait(barrier, NS - 1 + NG - 1 + (NY - 1) * (NZ - 1))
+    pl.semaphore_wait(barrier, NS - 1 + NG - 1)
 
     @pl.loop(1, NS)
     def _(k):
@@ -211,13 +204,6 @@
     for n in range(NEG):
         mask = mask + (slot_lane == to_column(slots[n], QD).astype(jnp.int32)).astype(F32)
     mask_v[...] = mask
-
-    local_copies[3].wait()
-
-    @pl.loop(0, TOK // 256)
-    def _(i):
-        at = pl.multiple_of(i * 256, 256)
-        xt_v[:, pl.ds(at, 256)] = x_v[pl.ds(at, 256), :].T
 
     def gather_rest(buf, rs, fs):
         @pl.loop(1, NY)
@@ -259,7 +245,9 @@
 
     send_rows(2, 0)
     send_rows(2, 1)
-
+    send_rows(3, 0)
+
+    local_copies[3].wait()
     local_copies[2].wait()
     gather_rest(ww_v, ww_rs, fw_ss)
 
@@ -275,7 +263,6 @@
         xx = (x + k) % NX
         remote(line, line, line_ss.at[k], line_rs.at[x], g, xx * NZ + z).start()
 
-    send_rows(3, 0)
     send_rows(3, 1)
 
     @pl.loop(0, TOK // 256)
@@ -289,6 +276,11 @@
         qv_f[pl.ds(q_at, 8), :] = jnp.sum(hidden.reshape(8, QL, D), axis=1) * (1.0 / QL)
 
     qv_v[...] = qv_f[...].astype(BF)
+
+    @pl.loop(0, TOK // 256)
+    def _(i):
+        at = pl.multiple_of(i * 256, 256)
+        xt_v[:, pl.ds(at, 256)] = x_v[pl.ds(at, 256), :].T
 
     def score(i):
         xx = (x + NX - i) % NX
@@ -514,10 +506,8 @@
 
     f_l[g] = f_s[...]
 
-    @pl.loop(1, NG)
-    def _(k):
-        gg = (g + k) % NG
-        remote(f_s, f_l.at[g], f_ss.at[k], f_rs.at[g], gg, s).start()
+    for k in (4, 5, 3, 2, 6, 1, 7):
+        remote(f_s, f_l.at[g], f_ss.at[k], f_rs.at[g], (g + k) % NG, s).start()
 
     @pl.loop(0, NX)
     def _(i):

time: 95.5 us -> 94.8 us (level)
  no operation moved by 1% of the time
where the time goes in v5:
time: 94.8 us; the launch traced here: 94.6 us
  Pallas kernels  94 us (99%)
    pallas_call x1, Pallas kernels, shards(): pl.pallas_call(kernel, out_shape=(jax.ShapeDtypeStruct((NG, 32, 128), BF)...  92.5 us

profile of v5, /device:TPU:1, one launch (start us, length us, event | category | flops | bytes accessed | tf_op | source)
XLA Modules:
  0.0 94.6 jit_solution(12817078381508215816)
XLA Ops:
  0.6 92.5 %retriever_step.1 = (bf16[8,32,128]{2,1,0:T(8,128)(2,1)}, f32[1,64]{1,0:T(1,128)}, bf16[32,128]{1,0:T(8,128)(2,1)}) custom-call(s32[8,1,64]{2,1,0:T(1,128)} %bitcast.8, s32[8,64]{1,0:T(8,128)} %bitcast.9, s32[1,64]{1,0:T(1,128)} %bitcast.10, bf16[2048,1024]{1,0:T(8,128)(2,1)} %bitcast.6, bf16[512,1024]{1,0:T(8,128)(2,1)} %bitcast.7, ...), custom_call_target="tpu_custom_call" | custom-call | flops 17179869184 | bytes 12582912 | tf_op jit(solution)/shard_map/retriever_step/pallas_call | solution.py:616
  93.1 1.5 %hand_over.1 = (f32[32,1024]{1,0:T(8,128)}, f32[1,64]{1,0:T(1,128)}, bf16[4,1024]{1,0:T(4,128)(2,1)}) custom-call(bf16[8,32,128]{2,1,0:T(8,128)(2,1)} %get-tuple-element.9.grad, f32[1,64]{1,0:T(1,128)} %get-tuple-element.10.loss, bf16[32,128]{1,0:T(8,128)(2,1)} %get-tuple-element.11.emb), custom_call_target="tpu_custom_call" | custom-call | tf_op jit(solution)/shard_map/hand_over/pallas_call | solution.py:643

commit v6 on v5

--- a/solution.py
+++ b/solution.py
@@ -282,6 +282,21 @@
         at = pl.multiple_of(i * 256, 256)
         xt_v[:, pl.ds(at, 256)] = x_v[pl.ds(at, 256), :].T
 
+    @pl.loop(1, NS)
+    def _(k):
+        o = (s + k) % NS
+        wait_out(req_s.at[o], req_ss.at[o])
+
+    for buf, ss, fs in ((wp_v, wp_ss, fp_ss), (ww_v, ww_ss, fw_ss)):
+
+        @pl.loop(0, NY)
+        def _(k):
+            wait_out(buf.at[g], ss.at[k])
+
+        @pl.loop(1, NY)
+        def _(k):
+            wait_out(buf.at[((y + k) % NY) * NC + c], fs.at[k])
+
     def score(i):
         xx = (x + NX - i) % NX
 
@@ -360,14 +375,15 @@
         part_a, part_b = both[:RA], both[RA:]
         acc_b[xx] = part_b
         b_s[xx] = part_b.astype(BF)
+
+        @pl.when(i < NX - 1)
+        def _():
+            remote(b_s.at[xx], b_l.at[i], b_ss.at[i], b_rs.at[i], g, xx * NZ + z).start()
+
         for k in range(NY):
             piece = part_a[:, k * 128 : (k + 1) * 128]
             acc_a[k, xx] = piece
             a_s[k, xx] = piece.astype(BF)
-
-        @pl.when(i < NX - 1)
-        def _():
-            remote(b_s.at[xx], b_l.at[i], b_ss.at[i], b_rs.at[i], g, xx * NZ + z).start()
 
         @pl.loop(1, NY)
         def _(k):
@@ -453,7 +469,6 @@
     @pl.loop(1, NS)
     def _(k):
         o = (s + k) % NS
-        wait_out(req_s.at[o], req_ss.at[o])
         wait_out(found.at[0, 0, 0], row_ss.at[o])
 
     @pl.loop(1, NZ)
@@ -463,16 +478,6 @@
     @pl.loop(1, NX)
     def _(k):
         wait_out(emb_l.at[pl.ds(0, NZ)], line_ss.at[k])
-
-    for buf, ss, fs in ((wp_v, wp_ss, fp_ss), (ww_v, ww_ss, fw_ss)):
-
-        @pl.loop(0, NY)
-        def _(k):
-            wait_out(buf.at[g], ss.at[k])
-
-        @pl.loop(1, NY)
-        def _(k):
-            wait_out(buf.at[((y + k) % NY) * NC + c], fs.at[k])
 
     @pl.loop(0, NX)
     def _(i):

time: 94.8 us -> 94.8 us (level)
  no operation moved by 1% of the time
where the time goes in v6:
time: 94.8 us; the launch traced here: 94.6 us
  Pallas kernels  94 us (99%)
    pallas_call x1, Pallas kernels, shards(): pl.pallas_call(kernel, out_shape=(jax.ShapeDtypeStruct((NG, 32, 128), BF)...  92.4 us

profile of v6, /device:TPU:1, one launch (start us, length us, event | category | flops | bytes accessed | tf_op | source)
XLA Modules:
  0.0 94.6 jit_solution(13184914285892839701)
XLA Ops:
  0.6 92.4 %retriever_step.1 = (bf16[8,32,128]{2,1,0:T(8,128)(2,1)}, f32[1,64]{1,0:T(1,128)}, bf16[32,128]{1,0:T(8,128)(2,1)}) custom-call(s32[8,1,64]{2,1,0:T(1,128)} %bitcast.8, s32[8,64]{1,0:T(8,128)} %bitcast.9, s32[1,64]{1,0:T(1,128)} %bitcast.10, bf16[2048,1024]{1,0:T(8,128)(2,1)} %bitcast.6, bf16[512,1024]{1,0:T(8,128)(2,1)} %bitcast.7, ...), custom_call_target="tpu_custom_call" | custom-call | flops 17179869184 | bytes 12582912 | tf_op jit(solution)/shard_map/retriever_step/pallas_call | solution.py:621
  93.1 1.5 %hand_over.1 = (f32[32,1024]{1,0:T(8,128)}, f32[1,64]{1,0:T(1,128)}, bf16[4,1024]{1,0:T(4,128)(2,1)}) custom-call(bf16[8,32,128]{2,1,0:T(8,128)(2,1)} %get-tuple-element.9.grad, f32[1,64]{1,0:T(1,128)} %get-tuple-element.10.loss, bf16[32,128]{1,0:T(8,128)(2,1)} %get-tuple-element.11.emb), custom_call_target="tpu_custom_call" | custom-call | tf_op jit(solution)/shard_map/hand_over/pallas_call | solution.py:648
